TPU v7x, 32 devices: a whole 2x2x4 slice. The times are simulated.
32 devices in a mesh: rec: 4 (over y, core), tract: 8 (over z, x).
Axes of the slice: x: 2, y: 2, z: 4, core: 2. Of those that a mesh axis runs over, the one named last changes fastest.
Arguments:
- rep_weights: float32 [80, 131072], P(None, ('rec', 'tract')), may hold values from 0.5 to 2
- covariate_codes: int32 [5, 131072], P(None, ('rec', 'tract')), may hold values from 0 to 15
- tract_of: int32 [131072, 1], P(('rec', 'tract')), may hold values from 0 to 7; in each aligned block of 4096 rows (0 to 4095, 4096 to 8191, ...) at most 1536 rows name the same one
- log_income: bfloat16 [131072], P(('rec', 'tract')), may hold values from -5 to 5
- controls: float32 [64], replicated, may hold values from 7782 to 10240
- threshold_grid: int32 [2048], replicated, may hold values from 0 to 4095
Outputs:
- calibrated: float32 [80, 131072], P(None, ('rec', 'tract'))
- income_tables: float32 [8, 80, 2048], P('tract', None, 'rec')
Inputs may be any that keep to these rules, and one draw needn't show every extreme that they name: `tract_of`: among the 4096 persons of one device at most 1536 share a tract; in some aligned blocks of 4096 persons one tract has exactly 1536.
All inputs are finite; a program needn't handle non-finite values.
Results may differ from a plain program's by a relative error of at most 0.0003.
Values may be sent and summed in bfloat16 or wider, within the bound.
A program may use at most 128 MiB of HBM per device.

v0:
```python
import functools

import jax
import jax.numpy as jnp
from jax import lax
from jax.experimental import pallas as pl
from jax.experimental.pallas import tpu as pltpu
from jax.sharding import PartitionSpec as P

smooth_width = 3.0 / 8192.0
grid_middle = 2048.0
grid_step = 3.0 / 2048.0
base_levels = 16
first_kept = 4
vmem_bytes = 48 * 1024 * 1024
bf16 = jnp.bfloat16
f32 = jnp.float32


def pair_layout(variables):
    offsets, row = {}, 0
    for u in range(variables):
        first = 0 if u == 0 else first_kept
        for v in range(u + 1, variables):
            offsets[u, v] = row
            row += (base_levels - first) * base_levels
    singles = row
    row += variables * base_levels
    return offsets, singles, row


def split3(value, axis):
    high = value.astype(bf16)
    rest = value - high.astype(f32)
    middle = rest.astype(bf16)
    low = (rest - middle.astype(f32)).astype(bf16)
    return jnp.concatenate([high, middle, low], axis=axis)


def one_hot(key, rows):
    width = key.shape[1]
    row = lax.broadcasted_iota(jnp.int32, (rows, width), 0)
    return jnp.where(row == key, 1.0, 0.0).astype(bf16)


def gram_kernel(w_ref, codes_ref, out_ref, pairs, total):
    step = pl.program_id(0)
    variables, _ = codes_ref.shape
    reps = w_ref.shape[0]
    offsets, singles, rows = pair_layout(variables)

    @pl.when(step == 0)
    def _():
        total[...] = jnp.zeros_like(total)
        pairs[rows:, :] = jnp.zeros((pairs.shape[0] - rows, pairs.shape[1]), bf16)

    pieces = split3(w_ref[...], 0)
    for (u, v), row in offsets.items():
        first = 0 if u == 0 else first_kept
        key = (codes_ref[u : u + 1, :] - first) * base_levels + codes_ref[v : v + 1, :]
        count = (base_levels - first) * base_levels
        pairs[row : row + count, :] = one_hot(key, count)
    for v in range(variables):
        row = singles + v * base_levels
        pairs[row : row + base_levels, :] = one_hot(codes_ref[v : v + 1, :], base_levels)
    total[...] += lax.dot_general(
        pairs[...], pieces, (((1,), (1,)), ((), ())), preferred_element_type=f32
    )

    @pl.when(step == pl.num_programs(0) - 1)
    def _():
        out_ref[...] = (
            total[:, :reps] + total[:, reps : 2 * reps] + total[:, 2 * reps : 3 * reps]
        )


def gram(rep_weights, covariate_codes, multiple):
    reps, people = rep_weights.shape
    variables = covariate_codes.shape[0]
    rows = -(-pair_layout(variables)[2] // multiple) * multiple
    block = 1024
    return pl.pallas_call(
        gram_kernel,
        grid=(people // block,),
        in_specs=[
            pl.BlockSpec((reps, block), lambda i: (0, i)),
            pl.BlockSpec((variables, block), lambda i: (0, i)),
        ],
        out_specs=pl.BlockSpec((rows, reps), lambda i: (0, 0)),
        out_shape=jax.ShapeDtypeStruct((rows, reps), f32),
        scratch_shapes=[pltpu.VMEM((rows, block), bf16), pltpu.VMEM((rows, 3 * reps), f32)],
        compiler_params=pltpu.CompilerParams(vmem_limit_bytes=vmem_bytes),
        cost_estimate=pl.CostEstimate(
            flops=6 * rows * reps * people, bytes_accessed=4 * reps * people, transcendentals=0
        ),
    )(rep_weights, covariate_codes)


def solve_kernel(variables, sums_ref, controls_ref, out_ref, mat, rhs, coef, sol):
    size, _, reps = mat.shape
    offsets, singles, _ = pair_layout(variables)
    kept = base_levels - first_kept
    starts = [0] + [base_levels + kept * (v - 1) for v in range(1, variables)]
    firsts = [0] + [first_kept] * (variables - 1)
    mat[...] = jnp.zeros_like(mat)
    for v in range(variables):
        first, count = firsts[v], base_levels - firsts[v]
        single = sums_ref[singles + v * base_levels + first : singles + (v + 1) * base_levels, :]
        rhs[starts[v] : starts[v] + count, :] = (
            controls_ref[starts[v] : starts[v] + count, :] - single
        )
        for c in range(count):
            mat[starts[v] + c, starts[v] + c : starts[v] + c + 1, :] = single[c : c + 1, :]
    for (u, v), row in offsets.items():
        for c in range(base_levels - firsts[u]):
            at = row + c * base_levels + first_kept
            mat[starts[u] + c, starts[v] : starts[v] + kept, :] = sums_ref[at : at + kept, :]

    for block in range(size // 8):
        low = block * 8

        def eliminate(inner, carry, low=low, block=block):
            k = low + inner
            row = mat[k, low:, :]
            pivot = mat[k, pl.ds(k, 1), :]
            place = lax.broadcasted_iota(jnp.int32, row.shape, 0) + low
            factor = jnp.where(place > k, row * (1.0 / pivot), 0.0)
            coef[low:, :] = factor
            rhs[low:, :] = rhs[low:, :] - factor * rhs[pl.ds(k, 1), :]
            for other in range(block, size // 8):
                part = row[other * 8 - low :, :]
                for i in range(other * 8, other * 8 + 8):
                    mat[i, other * 8 :, :] = mat[i, other * 8 :, :] - coef[i : i + 1, :] * part
            return carry

        lax.fori_loop(0, 8, eliminate, 0)

    sol[...] = jnp.zeros_like(sol)
    for block in reversed(range(size // 8)):
        low = block * 8

        def substitute(inner, carry, low=low):
            k = low + 7 - inner
            known = jnp.sum(mat[k, low:, :] * sol[low:, :], axis=0, keepdims=True)
            sol[pl.ds(k, 1), :] = (rhs[pl.ds(k, 1), :] - known) / mat[k, pl.ds(k, 1), :]
            return carry

        lax.fori_loop(0, 8, substitute, 0)

    out_ref[...] = jnp.zeros_like(out_ref)
    for v in range(variables):
        count = base_levels - firsts[v]
        at = v * base_levels + firsts[v]
        out_ref[at : at + count, :] = sol[starts[v] : starts[v] + count, :]


def solve(sums, controls, variables):
    reps = sums.shape[1]
    size = controls.shape[0]
    return pl.pallas_call(
        functools.partial(solve_kernel, variables),
        in_specs=[pl.BlockSpec(memory_space=pltpu.VMEM)] * 2,
        out_specs=pl.BlockSpec(memory_space=pltpu.VMEM),
        out_shape=jax.ShapeDtypeStruct((variables * base_levels, reps), f32),
        scratch_shapes=[
            pltpu.VMEM((size, size, reps), f32),
            pltpu.VMEM((size, reps), f32),
            pltpu.VMEM((size, reps), f32),
            pltpu.VMEM((size, reps), f32),
        ],
        compiler_params=pltpu.CompilerParams(vmem_limit_bytes=vmem_bytes),
    )(sums, jnp.broadcast_to(controls[:, None], (size, reps)))


def calibrate_kernel(x_ref, w_ref, codes_ref, cal_ref, sent_ref):
    variables = codes_ref.shape[0]
    design = jnp.concatenate(
        [one_hot(codes_ref[v : v + 1, :], base_levels) for v in range(variables)], axis=0
    )
    pieces = split3(x_ref[...], 0)
    adjustment = lax.dot_general(
        pieces,
        jnp.concatenate([design] * 3, axis=0),
        (((0,), (0,)), ((), ())),
        preferred_element_type=f32,
    )
    calibrated = w_ref[...] * (1.0 + adjustment)
    cal_ref[...] = calibrated
    sent_ref[...] = calibrated.astype(bf16)


def calibrate(x, rep_weights, covariate_codes):
    reps, people = rep_weights.shape
    variables = covariate_codes.shape[0]
    block = 1024
    return pl.pallas_call(
        calibrate_kernel,
        grid=(people // block,),
        in_specs=[
            pl.BlockSpec(x.shape, lambda i: (0, 0)),
            pl.BlockSpec((reps, block), lambda i: (0, i)),
            pl.BlockSpec((variables, block), lambda i: (0, i)),
        ],
        out_specs=[pl.BlockSpec((reps, block), lambda i: (0, i))] * 2,
        out_shape=[
            jax.ShapeDtypeStruct((reps, people), f32),
            jax.ShapeDtypeStruct((reps, people), bf16),
        ],
        compiler_params=pltpu.CompilerParams(vmem_limit_bytes=vmem_bytes),
    )(x, rep_weights, covariate_codes)


def table_kernel(tracts, sent_ref, about_ref, grid_ref, out_ref, masked):
    step = pl.program_id(0) * pl.num_programs(1) + pl.program_id(1)
    reps = sent_ref.shape[1]
    sent = sent_ref[0]
    income = about_ref[0, 0:1, :]
    tract = about_ref[0, 1:2, :]
    for k in range(tracts):
        inside = jnp.where(tract == float(k), 1.0, 0.0).astype(bf16)
        masked[k * reps : (k + 1) * reps, :] = sent * inside
    centers = (grid_ref[...].astype(f32) - grid_middle) * grid_step
    half = (centers - income) * (0.5 / smooth_width)
    smoothed = (0.5 + 0.5 * jnp.tanh(half)).astype(bf16)
    product = lax.dot_general(
        masked[...], smoothed, (((1,), (1,)), ((), ())), preferred_element_type=f32
    )

    @pl.when(step == 0)
    def _():
        out_ref[...] = product

    @pl.when(step > 0)
    def _():
        out_ref[...] += product


def partial_tables(sent, about, grid_column, tracts):
    sources, reps, people = sent.shape
    thresholds = grid_column.shape[0]
    block = 1024
    return pl.pallas_call(
        functools.partial(table_kernel, tracts),
        grid=(sources, people // block),
        in_specs=[
            pl.BlockSpec((1, reps, block), lambda s, i: (s, 0, i)),
            pl.BlockSpec((1, 2, block), lambda s, i: (s, 0, i)),
            pl.BlockSpec((thresholds, 1), lambda s, i: (0, 0)),
        ],
        out_specs=pl.BlockSpec((tracts * reps, thresholds), lambda s, i: (0, 0)),
        out_shape=jax.ShapeDtypeStruct((tracts * reps, thresholds), f32),
        scratch_shapes=[pltpu.VMEM((tracts * reps, block), bf16)],
        compiler_params=pltpu.CompilerParams(vmem_limit_bytes=vmem_bytes),
    )(sent, about, grid_column)


def greet(axes):
    barrier = pltpu.get_barrier_semaphore()
    count = 0
    for name, size in axes:
        me = lax.axis_index(name)
        for d in range(1, size):
            pl.semaphore_signal(
                barrier,
                inc=1,
                device_id={name: lax.rem(me + d, size)},
                device_id_type=pl.DeviceIdType.MESH,
            )
            count += 1
    pl.semaphore_wait(barrier, count)


def send(source, target, sems, slot, name, peer):
    copy = pltpu.make_async_remote_copy(
        src_ref=source,
        dst_ref=target,
        send_sem=sems.at[0, slot],
        recv_sem=sems.at[1, slot],
        device_id={name: peer},
        device_id_type=pl.DeviceIdType.MESH,
    )
    copy.start()
    return copy


def total_kernel(
    recs, tracts, x_ref, about_ref, out_ref, around_ref, from_rec, part, from_tract,
    about_sems, rec_sems, tract_sems, tract_back, rec_back,
):
    rec, tract = lax.axis_index("rec"), lax.axis_index("tract")
    large, small = part.shape[0], from_tract.shape[1]
    greet([("rec", recs), ("tract", tracts)])

    arriving = []
    for d in range(1, recs):
        peer = lax.rem(rec + d, recs)
        rows = pl.ds(pl.multiple_of(peer * large, 8), large)
        arriving.append(send(x_ref.at[rows], from_rec.at[d], rec_sems, d, "rec", peer))
    about = []
    for d in range(1, recs):
        peer = lax.rem(rec + d, recs)
        about.append(send(about_ref, around_ref.at[rec], about_sems, d, "rec", peer))
    around_ref[rec] = about_ref[...]
    for copy in arriving:
        copy.wait()
    value = x_ref[pl.ds(pl.multiple_of(rec * large, 8), large), :]
    for d in range(1, recs):
        value = value + from_rec[d]
    part[...] = value

    arriving = []
    for d in range(1, tracts):
        peer = lax.rem(tract + d, tracts)
        rows = pl.ds(pl.multiple_of(peer * small, 8), small)
        arriving.append(send(part.at[rows], from_tract.at[d], tract_sems, d, "tract", peer))
    for copy in arriving:
        copy.wait()
    value = part[pl.ds(pl.multiple_of(tract * small, 8), small), :]
    for d in range(1, tracts):
        value = value + from_tract[d]
    mine = pl.ds(pl.multiple_of(rec * large + tract * small, 8), small)
    out_ref[mine, :] = value

    arriving = []
    for d in range(1, tracts):
        peer = lax.rem(tract + d, tracts)
        arriving.append(send(out_ref.at[mine], out_ref.at[mine], tract_back, d, "tract", peer))
    for copy in arriving:
        copy.wait()
    mine = pl.ds(pl.multiple_of(rec * large, 8), large)
    arriving = []
    for d in range(1, recs):
        peer = lax.rem(rec + d, recs)
        arriving.append(send(out_ref.at[mine], out_ref.at[mine], rec_back, d, "rec", peer))
    for copy in arriving + about:
        copy.wait()


def totals(x, about, recs, tracts):
    rows, reps = x.shape
    large, small = rows // recs, rows // (recs * tracts)
    dma = pltpu.SemaphoreType.DMA
    return pl.pallas_call(
        functools.partial(total_kernel, recs, tracts),
        in_specs=[pl.BlockSpec(memory_space=pltpu.VMEM)] * 2,
        out_specs=[pl.BlockSpec(memory_space=pltpu.VMEM)] * 2,
        out_shape=[
            jax.ShapeDtypeStruct((rows, reps), f32),
            jax.ShapeDtypeStruct((recs,) + about.shape, f32),
        ],
        scratch_shapes=[
            pltpu.VMEM((recs, large, reps), f32),
            pltpu.VMEM((large, reps), f32),
            pltpu.VMEM((tracts, small, reps), f32),
            dma((2, recs)),
            dma((2, recs)),
            dma((2, tracts)),
            dma((2, tracts)),
            dma((2, recs)),
        ],
        compiler_params=pltpu.CompilerParams(
            vmem_limit_bytes=vmem_bytes, collective_id=0, has_side_effects=True
        ),
    )(x, about)


def scatter_kernel(tracts, scale, x_ref, out_ref, landed, sems):
    tract = lax.axis_index("tract")
    reps = out_ref.shape[1]
    greet([("tract", tracts)])
    arriving = []
    for d in range(1, tracts):
        peer = lax.rem(tract + d, tracts)
        rows = pl.ds(pl.multiple_of(peer * reps, 8), reps)
        arriving.append(send(x_ref.at[rows], landed.at[d], sems, d, "tract", peer))
    value = x_ref[pl.ds(pl.multiple_of(tract * reps, 8), reps), :]
    for d in range(1, tracts):
        arriving[d - 1].wait()
        value = value + landed[d]
    out_ref[0] = value / scale


def scatter(x, reps, tracts, scale):
    columns = x.shape[1]
    return pl.pallas_call(
        functools.partial(scatter_kernel, tracts, scale),
        in_specs=[pl.BlockSpec(memory_space=pltpu.VMEM)],
        out_specs=pl.BlockSpec(memory_space=pltpu.VMEM),
        out_shape=jax.ShapeDtypeStruct((1, reps, columns), f32),
        scratch_shapes=[
            pltpu.VMEM((tracts, reps, columns), f32),
            pltpu.SemaphoreType.DMA((2, tracts)),
        ],
        compiler_params=pltpu.CompilerParams(
            vmem_limit_bytes=vmem_bytes, collective_id=1, has_side_effects=True
        ),
    )(x)


def shards(rep_weights, covariate_codes, tract_of, log_income, controls, threshold_grid):
    reps, people = rep_weights.shape
    variables = covariate_codes.shape[0]
    tracts = lax.axis_size("tract")
    recs = lax.axis_size("rec")
    share = threshold_grid.shape[0] // recs
    grid_column = lax.dynamic_slice_in_dim(
        threshold_grid, lax.axis_index("rec") * share, share, 0
    )[:, None]
    about = jnp.stack([log_income.astype(f32), tract_of[:, 0].astype(f32)])
    sums = gram(rep_weights, covariate_codes, 8 * recs * tracts)
    sums, about = totals(sums, about, recs, tracts)
    x = solve(sums, controls, variables)
    calibrated, sent = calibrate(x, rep_weights, covariate_codes)
    sent = lax.all_gather(sent, "rec")
    tables = partial_tables(sent, about, grid_column, tracts)
    return calibrated, scatter(tables, reps, tracts, float(people * recs))


def solution(mesh):
    placed = (
        P(None, ("rec", "tract")),
        P(None, ("rec", "tract")),
        P(("rec", "tract"), None),
        P(("rec", "tract")),
        P(),
        P(),
    )
    return jax.shard_map(
        shards,
        mesh=mesh,
        in_specs=placed,
        out_specs=(P(None, ("rec", "tract")), P("tract", None, "rec")),
        check_vma=False,
    )
```

profile of v0, /device:TPU:11, one launch (start us, length us, event | category | flops | bytes accessed | tf_op | source)
XLA Modules:
  0.0 162.6 jit_solution(5301677454327253195)
XLA Ops:
  7.2 0.0 all-gather.3.cloned.1.call-start
  7.2 0.7 convert_bitcast_fusion
  7.9 0.7 stack.13
  8.7 0.0 copy-start.1
  8.7 1.3 copy-done.1
  10.0 0.0 copy-start.3
  10.0 0.9 copy-done.3
  10.9 0.0 copy-start.4
  10.9 8.5 %shard_map.77.x_ref = f32[2304,80]{1,0:T(8,128)S(1)} custom-call(f32[80,4096]{1,0:T(8,128)S(1)} %copy-done.1, s32[5,4096]{1,0:T(8,128)S(1)} %copy-done.3), custom_call_target="tpu_custom_call" | custom-call | flops 4529848320 | bytes 1310720 | tf_op jit(solution)/shard_map/pallas_call | solution.py:82
  19.4 0.0 copy-start.2
  19.4 47.7 %shard_map.78 = (f32[2304,80]{1,0:T(8,128)S(1)}, f32[4,2,4096]{2,1,0:T(2,128)S(1)}) custom-call(f32[2304,80]{1,0:T(8,128)S(1)} %shard_map.77.x_ref, f32[2,4096]{1,0:T(2,128)S(1)} %pad_maximum_fusion.about_ref), custom_call_target="tpu_custom_call" | custom-call | tf_op jit(solution)/shard_map/pallas_call | solution.py:343
  67.1 0.0 copy-done.4
  67.1 0.1 broadcast_in_dim.4.controls_ref
  67.2 5.4 %shard_map.79.x_ref = f32[80,80]{1,0:T(8,128)S(1)} custom-call(f32[2304,80]{1,0:T(8,128)S(1)} %get-tuple-element.6.sums_ref, f32[64,80]{1,0:T(8,128)S(1)} %broadcast_in_dim.4.controls_ref), custom_call_target="tpu_custom_call" | custom-call | tf_op jit(solution)/shard_map/pallas_call | solution.py:160
  72.6 0.0 copy-done.2
  72.6 2.4 %shard_map.80 = (f32[80,4096]{1,0:T(8,128)}, bf16[80,4096]{1,0:T(8,128)(2,1)}) custom-call(f32[80,80]{1,0:T(8,128)S(1)} %shard_map.79.x_ref, f32[80,4096]{1,0:T(8,128)S(1)} %copy-done.2, s32[5,4096]{1,0:T(8,128)S(1)} %copy-done.3), custom_call_target="tpu_custom_call" | custom-call | tf_op jit(solution)/shard_map/pallas_call | solution.py:196
  75.1 0.0 all-gather.3.cloned.1.call-update
  75.1 0.8 dynamic_slice.3
  75.9 0.1 copy.8.grid_ref
  76.0 25.7 %all-gather.3.cloned.1.call-done = bf16[320,4096]{1,0:T(8,128)(2,1)} async-done(((bf16[80,4096]{1,0:T(8,128)(2,1)}), bf16[320,4096]{1,0:T(8,128)(2,1)}) %all-gather.3.cloned.1.call-update) | async-done | bytes 2621456 | tf_op jit(solution)/shard_map/all_gather | solution.py:414
  101.8 0.0 copy-start
  101.8 1.7 %copy-done = bf16[320,4096]{1,0:T(8,128)(2,1)S(1)} copy-done((bf16[320,4096]{1,0:T(8,128)(2,1)S(1)}, bf16[320,4096]{1,0:T(8,128)(2,1)}, u32[]{:S(2)}) %copy-start) | copy-done | bytes 2621464
  103.5 18.8 %shard_map.81.x_ref = f32[640,512]{1,0:T(8,128)S(1)} custom-call(bf16[4,80,4096]{2,1,0:T(8,128)(2,1)S(1)} %bitcast.5, f32[4,2,4096]{2,1,0:T(2,128)S(1)} %get-tuple-element.9.about_ref, s32[512,1]{1,0:T(8,128)S(1)} %copy.8.grid_ref), custom_call_target="tpu_custom_call" | custom-call | tf_op jit(solution)/shard_map/pallas_call | solution.py:242
  122.3 32.8 %shard_map.82 = f32[1,80,512]{2,1,0:T(8,128)S(1)} custom-call(f32[640,512]{1,0:T(8,128)S(1)} %shard_map.81.x_ref), custom_call_target="tpu_custom_call" | custom-call | tf_op jit(solution)/shard_map/pallas_call | solution.py:385
  155.1 0.7 copy.10
  (1 shorter events, 0.0 us)
Async XLA Ops:
  7.2 94.6 %all-gather.3.cloned.1.call-start = ((), (), s32[]{:S(2)}) async-start(), calls=%async_computation | async-start | bytes 3276800 | tf_op jit(solution)/shard_map/all_gather | solution.py:414
  8.7 1.3 copy-start.1
  10.0 0.9 copy-start.3
  10.9 56.2 %copy-start.4 = (f32[64]{0:T(128)S(1)}, f32[64]{0:T(128)}, u32[]{:S(2)}) copy-start(f32[64]{0:T(128)} %param.10) | copy-start | bytes 772
  19.4 53.2 %copy-start.2 = (f32[80,4096]{1,0:T(8,128)S(1)}, f32[80,4096]{1,0:T(8,128)}, u32[]{:S(2)}) copy-start(f32[80,4096]{1,0:T(8,128)} %w_ref.3) | copy-start | bytes 3932164
  101.8 1.7 %copy-start = (bf16[320,4096]{1,0:T(8,128)(2,1)S(1)}, bf16[320,4096]{1,0:T(8,128)(2,1)}, u32[]{:S(2)}) copy-start(bf16[320,4096]{1,0:T(8,128)(2,1)} %all-gather.3.cloned.1.call-done) | copy-start | bytes 7864324
Sparse Core Ops, SparseCore 0:
  75.2 26.5 all-gather.2
where the time goes:
time: 163 us
  Pallas kernels  116 us (71%)
  waiting for transfers between devices  25.8 us (16%)
  between operations  14.1 us (9%)
  local copies, waits for them, and re-layouts  5.62 us (3%)
    pallas_call x1, Pallas kernels, totals(): pl.pallas_call(functools.partial(total_kernel, recs, tracts), in_specs=[p...  47.7 us
    pallas_call x1, Pallas kernels, scatter(): pl.pallas_call(functools.partial(scatter_kernel, tracts, scale), in_specs...  32.8 us
    all_gather x1, waiting for transfers between devices, shards(): sent = lax.all_gather(sent, 'rec')  25.7 us
    pallas_call x1, Pallas kernels, partial_tables(): pl.pallas_call(functools.partial(table_kernel, tracts), grid=(sources, pe...  18.8 us
    pallas_call x1, Pallas kernels, gram(): pl.pallas_call(gram_kernel, grid=(people // block,), in_specs=[pl.BlockSp...  8.47 us
    pallas_call x1, Pallas kernels, solve(): pl.pallas_call(functools.partial(solve_kernel, variables), in_specs=[pl.B...  5.44 us
    unnamed x11, local copies, waits for them, and re-layouts  4.63 us
  transfers between devices with their start and end apart: 1, of which 1 were waited for; matrix products, arithmetic and copies ran while one was open for 1% of the time, Pallas kernels for 0%

commit v1 on v0

v1 whole, which is shorter than its diff:
```python
import functools

import jax
import jax.numpy as jnp
from jax import lax
from jax.experimental import pallas as pl
from jax.experimental.pallas import tpu as pltpu
from jax.sharding import PartitionSpec as P

smooth_width = 3.0 / 8192.0
grid_middle = 2048.0
grid_step = 3.0 / 2048.0
half_scale = 0.5 / smooth_width
base_levels = 16
first_kept = 4
kept = base_levels - first_kept
lanes = 128
bf16 = jnp.bfloat16
f32 = jnp.float32
vmem_bytes = 60 * 1024 * 1024


def firsts_of(variables):
    return [0] + [first_kept] * (variables - 1)


def pair_layout(variables):
    offsets, row = {}, 0
    for u, first in enumerate(firsts_of(variables)):
        for v in range(u + 1, variables):
            offsets[u, v] = row
            row += (base_levels - first) * kept
    return offsets, row, row + base_levels


def split3(value, axis):
    high = value.astype(bf16)
    rest = value - high.astype(f32)
    middle = rest.astype(bf16)
    low = (rest - middle.astype(f32)).astype(bf16)
    return jnp.concatenate([high, middle, low], axis=axis)


def one_hot(key, rows):
    row = lax.broadcasted_iota(jnp.int32, (rows, key.shape[1]), 0)
    return jnp.where(row == key, 1.0, 0.0).astype(bf16)


def remote(source, target, send_sem, recv_sem, where):
    return pltpu.make_async_remote_copy(
        src_ref=source,
        dst_ref=target,
        send_sem=send_sem,
        recv_sem=recv_sem,
        device_id=where,
        device_id_type=pl.DeviceIdType.MESH,
    )


def solve(variables, sums, controls_ref, mat, rhs, coef, sol):
    size = mat.shape[0]
    offsets, singles, _ = pair_layout(variables)
    firsts = firsts_of(variables)
    starts = [0] + [base_levels + kept * (v - 1) for v in range(1, variables)]
    mat[...] = jnp.zeros_like(mat)
    for v in range(variables):
        count = base_levels - firsts[v]
        if v == 0:
            single = sums[singles : singles + count, :]
        else:
            at = offsets[0, v]
            single = sums[at : at + kept, :]
            for c in range(1, base_levels):
                single = single + sums[at + c * kept : at + (c + 1) * kept, :]
        rhs[starts[v] : starts[v] + count, :] = (
            controls_ref[starts[v] : starts[v] + count, :] - single
        )
        for c in range(count):
            mat[starts[v] + c, starts[v] + c : starts[v] + c + 1, :] = single[c : c + 1, :]
    for (u, v), row in offsets.items():
        for c in range(base_levels - firsts[u]):
            at = row + c * kept
            mat[starts[u] + c, starts[v] : starts[v] + kept, :] = sums[at : at + kept, :]

    for block in range(size // 8):
        low = block * 8

        def eliminate(inner, carry, low=low, block=block):
            k = low + inner
            row = mat[k, low:, :]
            pivot = mat[k, pl.ds(k, 1), :]
            place = lax.broadcasted_iota(jnp.int32, row.shape, 0) + low
            factor = jnp.where(place > k, row * (1.0 / pivot), 0.0)
            coef[low:, :] = factor
            rhs[low:, :] = rhs[low:, :] - factor * rhs[pl.ds(k, 1), :]
            for other in range(block, size // 8):
                part = row[other * 8 - low :, :]
                for i in range(other * 8, other * 8 + 8):
                    mat[i, other * 8 :, :] = mat[i, other * 8 :, :] - coef[i : i + 1, :] * part
            return carry

        lax.fori_loop(0, 8, eliminate, 0)

    sol[...] = jnp.zeros_like(sol)
    for block in reversed(range(size // 8)):
        low = block * 8

        def substitute(inner, carry, low=low):
            k = low + 7 - inner
            known = jnp.sum(mat[k, low:, :] * sol[low:, :], axis=0, keepdims=True)
            sol[pl.ds(k, 1), :] = (rhs[pl.ds(k, 1), :] - known) / mat[k, pl.ds(k, 1), :]
            return carry

        lax.fori_loop(0, 8, substitute, 0)

    parts = []
    for v in range(variables):
        count = base_levels - firsts[v]
        if firsts[v]:
            parts.append(jnp.zeros((firsts[v], sol.shape[1]), f32))
        parts.append(sol[starts[v] : starts[v] + count, :])
    return jnp.concatenate(parts, axis=0)


gram_block = 1024
smooth_block = 512
table_block = 1024


def kernel(
    ny, tracts, nx, scale,
    w_ref, codes_ref, tract_ref, income_ref, controls_ref, grid_ref,
    cal_ref, tab_ref,
    pieces, pairs, acc, gram, from_sister, from_chip, final, sums, mat, rhs, coef, sol, x3,
    about, others, corner, cen, smooth, design, sent, masked, table, from_x, over_x, from_z,
    about_sems, other_sems, sister_sems, send_chip, recv_chip, send_back, recv_back,
    final_sems, x_sems, z_sems,
):
    reps, people = w_ref.shape
    variables = codes_ref.shape[0]
    nz = tracts // nx
    blocks = 2 * ny
    chips = ny * tracts
    half = reps // 2
    tiles = gram.shape[1]
    offsets, singles, rows = pair_layout(variables)
    firsts = firsts_of(variables)
    share = smooth.shape[0]
    width = share // 2

    rec, tract = lax.axis_index("rec"), lax.axis_index("tract")
    y, core = lax.div(rec, 2), lax.rem(rec, 2)
    z, x = lax.div(tract, nx), lax.rem(tract, nx)
    sister = {"rec": 2 * y + 1 - core}
    shift = tracts - 2
    chip = y * tracts + lax.rem(tract + shift, tracts)

    def chip_at(number):
        return {
            "rec": 2 * lax.div(number, tracts) + core,
            "tract": lax.rem(lax.rem(number, tracts) + tracts - shift, tracts),
        }

    def each_other(count, body):
        def step(d, carry):
            body(lax.rem(chip + d, count))
            return carry

        lax.fori_loop(1, count, step, 0)

    barrier = pltpu.get_barrier_semaphore()
    pl.semaphore_signal(barrier, inc=1, device_id=sister, device_id_type=pl.DeviceIdType.MESH)
    each_other(
        chips,
        lambda peer: pl.semaphore_signal(
            barrier, inc=1, device_id=chip_at(peer), device_id_type=pl.DeviceIdType.MESH
        ),
    )

    about[0, 0:variables, :] = codes_ref[...].astype(f32)
    about[0, variables : variables + 1, :] = tract_ref[...].astype(f32)
    about[0, variables + 1 : variables + 2, :] = income_ref[...].astype(f32)
    about[0, variables + 2 :, :] = jnp.zeros((about.shape[1] - variables - 2, people), f32)
    pieces[...] = split3(w_ref[...], 0)

    pl.semaphore_wait(barrier, chips)

    def spread(source, slot, sems):
        return [remote(source, slot(1), sems.at[0, 1], sems.at[1, 1], sister)] + [
            remote(
                source,
                slot(2 * e),
                sems.at[0, 2 * e],
                sems.at[1, 2 * e],
                {"rec": 2 * lax.rem(y - e + ny, ny) + core},
            )
            for e in range(1, ny)
        ]

    def relay(slot, sems):
        return [
            remote(
                slot(2 * e), slot(2 * e + 1), sems.at[0, 2 * e + 1], sems.at[1, 2 * e + 1], sister
            )
            for e in range(1, ny)
        ]

    about_slot = lambda b: about.at[b]
    other_slot = lambda b: others.at[b - 1]
    about_copies = spread(about.at[0], about_slot, about_sems)
    other_copies = spread(w_ref, other_slot, other_sems)
    for copy in about_copies:
        copy.start()
    for copy in other_copies:
        copy.start()

    cut = offsets[1, 2] // lanes
    chunks = [(0, cut), (cut, tiles)]

    def gram_chunk(first, last):
        low, high = first * lanes, last * lanes
        groups = []
        for (u, v), row in offsets.items():
            if low <= row < high:
                groups.append((u, v, row - low, (base_levels - firsts[u]) * kept))
        acc[:, : high - low] = jnp.zeros((acc.shape[0], high - low), f32)

        def body(i, carry):
            cols = pl.ds(pl.multiple_of(i * gram_block, gram_block), gram_block)
            for u, v, row, count in groups:
                right = codes_ref[v : v + 1, cols] - first_kept
                key = (codes_ref[u : u + 1, cols] - firsts[u]) * kept + right
                key = jnp.where(right < 0, -1, key)
                pairs[row : row + count, :] = one_hot(key, count)
            if low <= singles < high:
                pairs[singles - low : high - low, :] = one_hot(
                    codes_ref[0:1, cols], high - singles
                )
            acc[:, : high - low] += lax.dot_general(
                pieces[:, cols],
                pairs[: high - low, :],
                (((1,), (1,)), ((), ())),
                preferred_element_type=f32,
            )
            return carry

        lax.fori_loop(0, people // gram_block, body, 0)
        for t in range(first, last):
            at = slice((t - first) * lanes, (t - first + 1) * lanes)
            value = acc[:reps, at] + acc[reps : 2 * reps, at] + acc[2 * reps :, at]
            gram[0, t] = value[:half]
            gram[1, t] = value[half:]

    def to_sister(c):
        first, last = chunks[c]
        return remote(
            gram.at[1 - core, first:last],
            from_sister.at[first:last],
            sister_sems.at[0, c],
            sister_sems.at[1, c],
            sister,
        )

    def to_chips(c):
        first, last = chunks[c]
        to_sister(c).wait_recv()
        for t in range(first, last):
            gram[core, t] = gram[core, t] + from_sister[t]

        def start(peer):
            @pl.when((peer >= first) & (peer < last))
            def _():
                remote(
                    gram.at[core, peer],
                    from_chip.at[chip],
                    send_chip.at[peer],
                    recv_chip.at[chip],
                    chip_at(peer),
                ).start()

        each_other(chips, start)

    def smooth_part(b, first, last):
        def body(i, carry):
            start = pl.multiple_of(i * smooth_block, smooth_block)
            cols = pl.ds(start, smooth_block)
            there = pl.ds(pl.multiple_of(b * people + start, smooth_block), smooth_block)
            income = about[b, variables + 1 : variables + 2, cols] * half_scale
            centers = jnp.concatenate([cen[...]] * (smooth_block // lanes), axis=1)
            smooth[:, there] = (0.5 + 0.5 * jnp.tanh(centers - income)).astype(bf16)
            for v in range(variables):
                code = about[b, v : v + 1, cols].astype(jnp.int32)
                design[v * base_levels : (v + 1) * base_levels, there] = one_hot(code, base_levels)
            return carry

        lax.fori_loop(first, last, body, 0)

    steps = people // smooth_block

    gram_chunk(*chunks[0])
    to_sister(0).start()
    gram_chunk(*chunks[1])
    to_sister(1).start()
    to_chips(0)

    corner[...] = jnp.zeros_like(corner)
    count = share // lanes
    corner[:count, :] = (
        (grid_ref[pl.ds(rec * count, count), :].astype(f32) - grid_middle)
        * (grid_step * half_scale)
    )
    turned = corner[...].T
    for i in range(count):
        cen[i * lanes : (i + 1) * lanes, :] = jnp.broadcast_to(turned[:, i : i + 1], (lanes, lanes))

    about_relay = relay(about_slot, about_sems)
    to_chips(1)
    smooth_part(0, 0, steps)
    for e in range(1, ny):
        about_copies[e].wait_recv()
        about_relay[e - 1].start()

    @pl.when(chip < tiles)
    def _():
        each_other(
            chips,
            lambda peer: remote(
                gram.at[core, 0], from_chip.at[peer], send_chip.at[0], recv_chip.at[peer], sister
            ).wait_recv(),
        )
        total = lax.fori_loop(
            1,
            chips,
            lambda d, value: value + from_chip[lax.rem(chip + d, chips)],
            gram[core, chip],
        )
        final[core, chip] = total
        each_other(
            chips,
            lambda peer: remote(
                final.at[core, chip],
                final.at[core, chip],
                send_back.at[peer],
                recv_back.at[chip],
                chip_at(peer),
            ).start(),
        )

    about_copies[0].wait_recv()
    smooth_part(1, 0, steps)

    def hand_over(t):
        return remote(
            final.at[core, t], final.at[core, t], final_sems.at[0, t], final_sems.at[1, t], sister
        )

    def taken(t):
        return remote(
            final.at[core, t],
            final.at[1 - core, t],
            final_sems.at[0, t],
            final_sems.at[1, t],
            sister,
        )

    for t in range(tiles):
        @pl.when(chip != t)
        def _():
            remote(
                final.at[core, t], final.at[core, t], send_back.at[0], recv_back.at[t], sister
            ).wait_recv()

        hand_over(t).start()
    for e in range(1, ny):
        smooth_part(2 * e, 0, steps)
        about_relay[e - 1].wait_recv()
        smooth_part(2 * e + 1, 0, steps)
    for t in range(tiles):
        taken(t).wait_recv()
        whole = jnp.concatenate([final[0, t], final[1, t]], axis=0)
        sums[t * lanes : (t + 1) * lanes, :] = whole.T

    x3[...] = split3(solve(variables, sums, controls_ref, mat, rhs, coef, sol), 0)

    other_relay = relay(other_slot, other_sems)
    for e in range(1, ny):
        other_copies[e].wait_recv()
        other_relay[e - 1].start()

    def table_pass(part):
        table[part] = jnp.zeros(table.shape[1:], f32)
        for b in range(blocks):
            if part == 0 and b > 0:
                if b % 2 == 1:
                    (other_copies[0] if b == 1 else other_relay[b // 2 - 1]).wait_recv()

            def body(i, carry, b=b):
                start = pl.multiple_of(i * table_block, table_block)
                cols = pl.ds(start, table_block)
                there = pl.ds(pl.multiple_of(b * people + start, table_block), table_block)
                if part == 0:
                    adjustment = lax.dot_general(
                        x3[...],
                        jnp.concatenate([design[:, there]] * 3, axis=0),
                        (((0,), (0,)), ((), ())),
                        preferred_element_type=f32,
                    )
                    weights = w_ref[:, cols] if b == 0 else others[b - 1, :, cols]
                    calibrated = weights * (1.0 + adjustment)
                    if b == 0:
                        cal_ref[:, cols] = calibrated
                    sent[:, there] = calibrated.astype(bf16)
                own = about[b, variables : variables + 1, cols]
                value = sent[:, there]
                for k in range(tracts):
                    at = (k % nx * nz + k // nx) * reps
                    inside = jnp.where(own == float(k), 1.0, 0.0).astype(bf16)
                    masked[at : at + reps, :] = value * inside
                table[part] += lax.dot_general(
                    masked[...],
                    smooth[part * width : (part + 1) * width, there],
                    (((1,), (1,)), ((), ())),
                    preferred_element_type=f32,
                )
                return carry

            lax.fori_loop(0, people // table_block, body, 0)

    deep = nz * reps

    def across_x(part, e):
        to = lax.rem(x + e, nx)
        return remote(
            table.at[part, pl.ds(pl.multiple_of(to * deep, 8), deep)],
            from_x.at[part, e - 1],
            x_sems.at[0, part, e],
            x_sems.at[1, part, e],
            {"tract": z * nx + to},
        )

    def along_z(part, e):
        to = lax.rem(z + e, nz)
        return remote(
            over_x.at[part, pl.ds(pl.multiple_of(to * reps, 8), reps)],
            from_z.at[part, e - 1],
            z_sems.at[0, part, e],
            z_sems.at[1, part, e],
            {"tract": to * nx + x},
        )

    for part in range(2):
        table_pass(part)
        for e in range(1, nx):
            across_x(part, e).start()
    for part in range(2):
        value = table[part, pl.ds(pl.multiple_of(x * deep, 8), deep), :]
        for e in range(1, nx):
            across_x(part, e).wait_recv()
            value = value + from_x[part, e - 1]
        over_x[part] = value
        for e in range(1, nz):
            along_z(part, e).start()
    for part in range(2):
        value = over_x[part, pl.ds(pl.multiple_of(z * reps, 8), reps), :]
        for e in range(1, nz):
            along_z(part, e).wait_recv()
            value = value + from_z[part, e - 1]
        tab_ref[0, :, part * width : (part + 1) * width] = value / scale

    for copy in about_copies + about_relay + other_copies + other_relay:
        copy.wait_send()
    for c in range(2):
        to_sister(c).wait_send()

    def left(peer):
        @pl.when(peer < tiles)
        def _():
            remote(
                gram.at[core, peer], from_chip.at[chip], send_chip.at[peer], recv_chip.at[chip],
                chip_at(peer),
            ).wait_send()

        @pl.when(chip < tiles)
        def _():
            remote(
                final.at[core, chip], final.at[core, chip], send_back.at[peer], recv_back.at[chip],
                chip_at(peer),
            ).wait_send()

    each_other(chips, left)
    for t in range(tiles):
        hand_over(t).wait_send()
    for part in range(2):
        for e in range(1, nx):
            across_x(part, e).wait_send()
        for e in range(1, nz):
            along_z(part, e).wait_send()


def shards(rep_weights, covariate_codes, tract_of, log_income, controls, threshold_grid):
    reps, people = rep_weights.shape
    variables = covariate_codes.shape[0]
    tracts = lax.axis_size("tract")
    recs = lax.axis_size("rec")
    ny = recs // 2
    nz = 4
    nx = tracts // nz
    chips = ny * tracts
    share = threshold_grid.shape[0] // recs
    width = share // 2
    size = controls.shape[0]
    rows = pair_layout(variables)[2]
    tiles = -(-rows // lanes)
    cut = pair_layout(variables)[0][1, 2] // lanes
    most = max(cut, tiles - cut) * lanes
    designs = variables * base_levels
    vmem = pltpu.VMEM
    dma = pltpu.SemaphoreType.DMA
    return pl.pallas_call(
        functools.partial(kernel, ny, tracts, nx, float(people * recs)),
        in_specs=[pl.BlockSpec(memory_space=vmem)] * 6,
        out_specs=[pl.BlockSpec(memory_space=vmem)] * 2,
        out_shape=[
            jax.ShapeDtypeStruct((reps, people), f32),
            jax.ShapeDtypeStruct((1, reps, share), f32),
        ],
        scratch_shapes=[
            vmem((3 * reps, people), bf16),
            vmem((most, gram_block), bf16),
            vmem((3 * reps, most), f32),
            vmem((2, tiles, reps // 2, lanes), f32),
            vmem((tiles, reps // 2, lanes), f32),
            vmem((chips, reps // 2, lanes), f32),
            vmem((2, tiles, reps // 2, lanes), f32),
            vmem((tiles * lanes, reps), f32),
            vmem((size, size, reps), f32),
            vmem((size, reps), f32),
            vmem((size, reps), f32),
            vmem((size, reps), f32),
            vmem((3 * designs, reps), bf16),
            vmem((recs, 8, people), f32),
            vmem((recs - 1, reps, people), f32),
            vmem((8, lanes), f32),
            vmem((share, lanes), f32),
            vmem((share, recs * people), bf16),
            vmem((designs, recs * people), bf16),
            vmem((reps, recs * people), bf16),
            vmem((tracts * reps, table_block), bf16),
            vmem((2, tracts * reps, width), f32),
            vmem((2, nx - 1, nz * reps, width), f32),
            vmem((2, nz * reps, width), f32),
            vmem((2, nz - 1, reps, width), f32),
            dma((2, recs)),
            dma((2, recs)),
            dma((2, 2)),
            dma((tiles,)),
            dma((chips,)),
            dma((chips,)),
            dma((tiles,)),
            dma((2, tiles)),
            dma((2, 2, nx)),
            dma((2, 2, nz)),
        ],
        compiler_params=pltpu.CompilerParams(
            vmem_limit_bytes=vmem_bytes, collective_id=0, has_side_effects=True
        ),
    )(
        rep_weights,
        covariate_codes,
        tract_of.reshape(1, people),
        log_income.astype(f32).reshape(1, people),
        jnp.broadcast_to(controls[:, None], (size, reps)),
        threshold_grid.reshape(-1, lanes),
    )


def solution(mesh):
    placed = (
        P(None, ("rec", "tract")),
        P(None, ("rec", "tract")),
        P(("rec", "tract"), None),
        P(("rec", "tract")),
        P(),
        P(),
    )
    return jax.shard_map(
        shards,
        mesh=mesh,
        in_specs=placed,
        out_specs=(P(None, ("rec", "tract")), P("tract", None, "rec")),
        check_vma=False,
    )
```

time: 163 us -> 104 us (0.64)
  the two profiles are of different devices: /device:TPU:11 before, /device:TPU:0 now
where the time goes in v1:
time: 104 us; the launch traced here: 103 us
  Pallas kernels  96.2 us (92%)
  local copies, waits for them, and re-layouts  4.52 us (4%)
  other arithmetic  1.3 us (1%)
    pallas_call x1, Pallas kernels, shards(): pl.pallas_call(functools.partial(kernel, ny, tracts, nx, float(people * r...  96.2 us
    unnamed x4, local copies, waits for them, and re-layouts  3.18 us

profile of v1, /device:TPU:0, one launch (start us, length us, event | category | flops | bytes accessed | tf_op | source)
XLA Modules:
  0.0 102.7 jit_solution(8170294051830037992)
XLA Ops:
  0.6 1.3 %reshape.20 = f32[4096]{0:T(1024)} convert(bf16[4096]{0:T(1024)(128)(2,1)} %param.9) | non-fusion elementwise | flops 4096 | bytes 24576 | tf_op jit(solution)/shard_map/reshape | solution.py:571
  1.9 1.3 %broadcast_in_dim.2.controls_ref = f32[64,80]{1,0:T(8,128)} broadcast(f32[64]{0:T(128)} %param.10), dimensions={0} | broadcast | bytes 20736 | tf_op jit(solution)/shard_map/broadcast_in_dim | solution.py:572
  3.3 96.2 %shard_map.77 = (f32[80,4096]{1,0:T(8,128)}, f32[1,80,512]{2,1,0:T(8,128)}) custom-call(f32[80,4096]{1,0:T(8,128)} %w_ref.1, s32[5,4096]{1,0:T(8,128)} %codes_ref.1, s32[1,4096]{1,0:T(1,128)} %bitcast.4, f32[1,4096]{1,0:T(1,128)} %bitcast.3, f32[64,80]{1,0:T(8,128)} %broadcast_in_dim.2.controls_ref, s32[16,128]{1,0:T(8,128)} %bitcast.5), custom_call_target="tpu_custom_call" | custom-call | tf_op jit(solution)/shard_map/pallas_call | solution.py:519
  99.5 0.0 copy-start
  99.5 2.5 %copy.10 = f32[80,4096]{1,0:T(8,128)} copy(f32[80,4096]{1,0:T(8,128)} %get-tuple-element.4) | data formatting | bytes 2621440
  102.0 0.0 copy-done
  102.0 0.7 copy.11
Async XLA Ops:
  99.5 2.5 %copy-start = (f32[1,80,512]{2,1,0:T(8,128)S(1)}, f32[1,80,512]{2,1,0:T(8,128)}, u32[]{:S(2)}) copy-start(f32[1,80,512]{2,1,0:T(8,128)} %get-tuple-element.5) | copy-start | bytes 491524

commit v2 on v1

--- a/solution.py
+++ b/solution.py
@@ -124,7 +124,10 @@
 
 gram_block = 1024
 smooth_block = 512
-table_block = 1024
+quarter = 1024
+low_weight, high_weight = 0.5, 2.0
+code_step = (high_weight - low_weight) / 65535.0
+table_block = quarter
 
 
 def kernel(
@@ -132,7 +135,7 @@
     w_ref, codes_ref, tract_ref, income_ref, controls_ref, grid_ref,
     cal_ref, tab_ref,
     pieces, pairs, acc, gram, from_sister, from_chip, final, sums, mat, rhs, coef, sol, x3,
-    about, others, corner, cen, smooth, design, sent, masked, table, from_x, over_x, from_z,
+    about, coded, others, located, corner, cen, smooth, design, sent, masked, table, from_x, over_x, from_z,
     about_sems, other_sems, sister_sems, send_chip, recv_chip, send_back, recv_back,
     final_sems, x_sems, z_sems,
 ):
@@ -177,10 +180,16 @@
         ),
     )
 
-    about[0, 0:variables, :] = codes_ref[...].astype(f32)
-    about[0, variables : variables + 1, :] = tract_ref[...].astype(f32)
-    about[0, variables + 1 : variables + 2, :] = income_ref[...].astype(f32)
-    about[0, variables + 2 :, :] = jnp.zeros((about.shape[1] - variables - 2, people), f32)
+    located[0, 0:variables, :] = codes_ref[...].astype(f32)
+    located[0, variables : variables + 1, :] = tract_ref[...].astype(f32)
+    located[0, variables + 1 : variables + 2, :] = income_ref[...]
+    located[0, variables + 2 :, :] = jnp.zeros((located.shape[1] - variables - 2, people), f32)
+    about[0] = jnp.concatenate(
+        [located[0, :, : people // 2], located[0, :, people // 2 :]], axis=0
+    ).astype(bf16)
+    for q in range(people // quarter):
+        part = w_ref[:, q * quarter : (q + 1) * quarter]
+        coded[q] = jnp.round((part - low_weight) / code_step - 32768.0).astype(jnp.int32).astype(jnp.int16)
     pieces[...] = split3(w_ref[...], 0)
 
     pl.semaphore_wait(barrier, chips)
@@ -206,13 +215,28 @@
         ]
 
     about_slot = lambda b: about.at[b]
-    other_slot = lambda b: others.at[b - 1]
+    quarters = people // quarter
+
+    def other_slot(q):
+        return lambda b: others.at[b - 1, q]
+
     about_copies = spread(about.at[0], about_slot, about_sems)
-    other_copies = spread(w_ref, other_slot, other_sems)
-    for copy in about_copies:
+    other_copies = [
+        spread(coded.at[q], other_slot(q), other_sems.at[q]) for q in range(quarters)
+    ]
+    about_relay = relay(about_slot, about_sems)
+    other_relay = [relay(other_slot(q), other_sems.at[q]) for q in range(quarters)]
+    for copy in about_copies[1:] + about_copies[:1]:
         copy.start()
-    for copy in other_copies:
-        copy.start()
+
+    def start_over_y(first, last):
+        for q in range(first, last):
+            for copy in other_copies[q][1:]:
+                copy.start()
+
+    start_over_y(0, quarters // 2)
+    for q in range(quarters):
+        other_copies[q][0].start()
 
     cut = offsets[1, 2] // lanes
     chunks = [(0, cut), (cut, tiles)]
@@ -281,15 +305,20 @@
         each_other(chips, start)
 
     def smooth_part(b, first, last):
+        if b > 0:
+            value = about[b].astype(f32)
+            located[b, :, : people // 2] = value[: value.shape[0] // 2]
+            located[b, :, people // 2 :] = value[value.shape[0] // 2 :]
+
         def body(i, carry):
             start = pl.multiple_of(i * smooth_block, smooth_block)
             cols = pl.ds(start, smooth_block)
             there = pl.ds(pl.multiple_of(b * people + start, smooth_block), smooth_block)
-            income = about[b, variables + 1 : variables + 2, cols] * half_scale
+            income = located[b, variables + 1 : variables + 2, cols] * half_scale
             centers = jnp.concatenate([cen[...]] * (smooth_block // lanes), axis=1)
             smooth[:, there] = (0.5 + 0.5 * jnp.tanh(centers - income)).astype(bf16)
             for v in range(variables):
-                code = about[b, v : v + 1, cols].astype(jnp.int32)
+                code = located[b, v : v + 1, cols].astype(jnp.int32)
                 design[v * base_levels : (v + 1) * base_levels, there] = one_hot(code, base_levels)
             return carry
 
@@ -313,8 +342,8 @@
     for i in range(count):
         cen[i * lanes : (i + 1) * lanes, :] = jnp.broadcast_to(turned[:, i : i + 1], (lanes, lanes))
 
-    about_relay = relay(about_slot, about_sems)
     to_chips(1)
+    start_over_y(quarters // 2, quarters - 1)
     smooth_part(0, 0, steps)
     for e in range(1, ny):
         about_copies[e].wait_recv()
@@ -371,6 +400,7 @@
             ).wait_recv()
 
         hand_over(t).start()
+    start_over_y(quarters - 1, quarters)
     for e in range(1, ny):
         smooth_part(2 * e, 0, steps)
         about_relay[e - 1].wait_recv()
@@ -382,17 +412,18 @@
 
     x3[...] = split3(solve(variables, sums, controls_ref, mat, rhs, coef, sol), 0)
 
-    other_relay = relay(other_slot, other_sems)
-    for e in range(1, ny):
-        other_copies[e].wait_recv()
-        other_relay[e - 1].start()
+    for q in range(quarters):
+        for e in range(1, ny):
+            other_copies[q][e].wait_recv()
+            other_relay[q][e - 1].start()
 
     def table_pass(part):
         table[part] = jnp.zeros(table.shape[1:], f32)
         for b in range(blocks):
             if part == 0 and b > 0:
                 if b % 2 == 1:
-                    (other_copies[0] if b == 1 else other_relay[b // 2 - 1]).wait_recv()
+                    for q in range(quarters):
+                        (other_copies[q][0] if b == 1 else other_relay[q][b // 2 - 1]).wait_recv()
 
             def body(i, carry, b=b):
                 start = pl.multiple_of(i * table_block, table_block)
@@ -405,12 +436,16 @@
                         (((0,), (0,)), ((), ())),
                         preferred_element_type=f32,
                     )
-                    weights = w_ref[:, cols] if b == 0 else others[b - 1, :, cols]
+                    if b == 0:
+                        weights = w_ref[:, cols]
+                    else:
+                        code = others[b - 1, i].astype(jnp.int32).astype(f32)
+                        weights = (code + 32768.0) * code_step + low_weight
                     calibrated = weights * (1.0 + adjustment)
                     if b == 0:
                         cal_ref[:, cols] = calibrated
                     sent[:, there] = calibrated.astype(bf16)
-                own = about[b, variables : variables + 1, cols]
+                own = located[b, variables : variables + 1, cols]
                 value = sent[:, there]
                 for k in range(tracts):
                     at = (k % nx * nz + k // nx) * reps
@@ -467,7 +502,7 @@
             value = value + from_z[part, e - 1]
         tab_ref[0, :, part * width : (part + 1) * width] = value / scale
 
-    for copy in about_copies + about_relay + other_copies + other_relay:
+    for copy in about_copies + about_relay + sum(other_copies + other_relay, []):
         copy.wait_send()
     for c in range(2):
         to_sister(c).wait_send()
@@ -538,8 +573,10 @@
             vmem((size, reps), f32),
             vmem((size, reps), f32),
             vmem((3 * designs, reps), bf16),
+            vmem((recs, 16, people // 2), bf16),
+            vmem((people // quarter, reps, quarter), jnp.int16),
+            vmem((recs - 1, people // quarter, reps, quarter), jnp.int16),
             vmem((recs, 8, people), f32),
-            vmem((recs - 1, reps, people), f32),
             vmem((8, lanes), f32),
             vmem((share, lanes), f32),
             vmem((share, recs * people), bf16),
@@ -551,7 +588,7 @@
             vmem((2, nz * reps, width), f32),
             vmem((2, nz - 1, reps, width), f32),
             dma((2, recs)),
-            dma((2, recs)),
+            dma((people // quarter, 2, recs)),
             dma((2, 2)),
             dma((tiles,)),
             dma((chips,)),

time: 104 us -> 82.7 us (0.80); the launches traced: 103 us -> 82.5 us
  Pallas kernels: 96.2 us -> 76 us
    pallas_call x1, Pallas kernels: 96.2 us -> 76 us  [shards(): pl.pallas_call(functools.partial(kernel, ny, tracts, nx, float(people * r...]
where the time goes in v2:
time: 82.7 us; the launch traced here: 82.5 us
  Pallas kernels  76 us (92%)
  local copies, waits for them, and re-layouts  4.52 us (5%)
  other arithmetic  1.3 us (2%)
    pallas_call x1, Pallas kernels, shards(): pl.pallas_call(functools.partial(kernel, ny, tracts, nx, float(people * r...  76 us
    unnamed x4, local copies, waits for them, and re-layouts  3.18 us

profile of v2, /device:TPU:0, one launch (start us, length us, event | category | flops | bytes accessed | tf_op | source)
XLA Modules:
  0.0 82.5 jit_solution(6509324109062242662)
XLA Ops:
  0.6 1.3 %reshape.20 = f32[4096]{0:T(1024)} convert(bf16[4096]{0:T(1024)(128)(2,1)} %param.9) | non-fusion elementwise | flops 4096 | bytes 24576 | tf_op jit(solution)/shard_map/reshape | solution.py:608
  1.9 1.3 %broadcast_in_dim.2.controls_ref = f32[64,80]{1,0:T(8,128)} broadcast(f32[64]{0:T(128)} %param.10), dimensions={0} | broadcast | bytes 20736 | tf_op jit(solution)/shard_map/broadcast_in_dim | solution.py:609
  3.3 76.0 %shard_map.77 = (f32[80,4096]{1,0:T(8,128)}, f32[1,80,512]{2,1,0:T(8,128)}) custom-call(f32[80,4096]{1,0:T(8,128)} %w_ref.1, s32[5,4096]{1,0:T(8,128)} %codes_ref.1, s32[1,4096]{1,0:T(1,128)} %bitcast.4, f32[1,4096]{1,0:T(1,128)} %bitcast.3, f32[64,80]{1,0:T(8,128)} %broadcast_in_dim.2.controls_ref, s32[16,128]{1,0:T(8,128)} %bitcast.5), custom_call_target="tpu_custom_call" | custom-call | tf_op jit(solution)/shard_map/pallas_call | solution.py:554
  79.3 0.0 copy-start
  79.3 2.5 %copy.10 = f32[80,4096]{1,0:T(8,128)} copy(f32[80,4096]{1,0:T(8,128)} %get-tuple-element.4) | data formatting | bytes 2621440
  81.8 0.0 copy-done
  81.8 0.7 copy.11
Async XLA Ops:
  79.3 2.5 %copy-start = (f32[1,80,512]{2,1,0:T(8,128)S(1)}, f32[1,80,512]{2,1,0:T(8,128)}, u32[]{:S(2)}) copy-start(f32[1,80,512]{2,1,0:T(8,128)} %get-tuple-element.5) | copy-start | bytes 491524

commit v3 on v2

--- a/solution.py
+++ b/solution.py
@@ -57,7 +57,21 @@
     )
 
 
-def solve(variables, sums, controls_ref, mat, rhs, coef, sol):
+def encode(value):
+    top = jnp.max(jnp.max(jnp.abs(value), axis=0, keepdims=True), axis=1, keepdims=True)
+    power = jnp.ceil(jnp.log2(jnp.maximum(top, 1e-30)))
+    coded = jnp.round(value * (code_top * jnp.exp2(-power)))
+    power = jnp.broadcast_to(power, (16, value.shape[1]))
+    return jnp.concatenate([coded, power], axis=0).astype(jnp.int32).astype(jnp.int16)
+
+
+def decode(coded):
+    coded = coded.astype(jnp.int32).astype(f32)
+    reps = coded.shape[0] - 16
+    return coded[:reps] * (jnp.exp2(coded[reps : reps + 1]) * (1.0 / code_top))
+
+
+def solve(variables, sums, aims, mat, rhs, coef, sol):
     size = mat.shape[0]
     offsets, singles, _ = pair_layout(variables)
     firsts = firsts_of(variables)
@@ -73,7 +87,7 @@
             for c in range(1, base_levels):
                 single = single + sums[at + c * kept : at + (c + 1) * kept, :]
         rhs[starts[v] : starts[v] + count, :] = (
-            controls_ref[starts[v] : starts[v] + count, :] - single
+            aims[starts[v] : starts[v] + count, :] - single
         )
         for c in range(count):
             mat[starts[v] + c, starts[v] + c : starts[v] + c + 1, :] = single[c : c + 1, :]
@@ -123,19 +137,19 @@
 
 
 gram_block = 1024
-smooth_block = 512
 quarter = 1024
 low_weight, high_weight = 0.5, 2.0
 code_step = (high_weight - low_weight) / 65535.0
-table_block = quarter
+code_top = 32000.0
 
 
 def kernel(
-    ny, tracts, nx, scale,
+    ny, tracts, nx,
     w_ref, codes_ref, tract_ref, income_ref, controls_ref, grid_ref,
     cal_ref, tab_ref,
     pieces, pairs, acc, gram, from_sister, from_chip, final, sums, mat, rhs, coef, sol, x3,
-    about, coded, others, located, corner, cen, smooth, design, sent, masked, table, from_x, over_x, from_z,
+    about, coded, others, located, corner, cen, smooth, design, sent, masked, masked_too, table,
+    to_x, from_x, over_x, to_z, from_z,
     about_sems, other_sems, sister_sems, send_chip, recv_chip, send_back, recv_back,
     final_sems, x_sems, z_sems,
 ):
@@ -148,8 +162,9 @@
     tiles = gram.shape[1]
     offsets, singles, rows = pair_layout(variables)
     firsts = firsts_of(variables)
-    share = smooth.shape[0]
-    width = share // 2
+    share = smooth.shape[1]
+    pieces_j = share // lanes
+    quarters = people // quarter
 
     rec, tract = lax.axis_index("rec"), lax.axis_index("tract")
     y, core = lax.div(rec, 2), lax.rem(rec, 2)
@@ -180,19 +195,27 @@
         ),
     )
 
-    located[0, 0:variables, :] = codes_ref[...].astype(f32)
-    located[0, variables : variables + 1, :] = tract_ref[...].astype(f32)
-    located[0, variables + 1 : variables + 2, :] = income_ref[...]
-    located[0, variables + 2 :, :] = jnp.zeros((located.shape[1] - variables - 2, people), f32)
-    about[0] = jnp.concatenate(
-        [located[0, :, : people // 2], located[0, :, people // 2 :]], axis=0
-    ).astype(bf16)
-    for q in range(people // quarter):
+    income = income_ref[...].astype(f32)
+    for q in range(quarters):
+        cols = slice(q * quarter, (q + 1) * quarter)
+        located[q, 0:variables, :] = codes_ref[:, cols].astype(f32)
+        located[q, variables : variables + 1, :] = tract_ref[:, cols].astype(f32)
+        for i in range(quarter // lanes):
+            row = q * (quarter // lanes) + i
+            located[q, variables + 1 : variables + 2, i * lanes : (i + 1) * lanes] = income[
+                row : row + 1, :
+            ]
+        located[q, variables + 2 :, :] = jnp.zeros(
+            (located.shape[1] - variables - 2, quarter), f32
+        )
+    for q in range(quarters // 2):
+        about[0, :, q * quarter : (q + 1) * quarter] = jnp.concatenate(
+            [located[q], located[quarters // 2 + q]], axis=0
+        ).astype(bf16)
+    for q in range(quarters):
         part = w_ref[:, q * quarter : (q + 1) * quarter]
         coded[q] = jnp.round((part - low_weight) / code_step - 32768.0).astype(jnp.int32).astype(jnp.int16)
     pieces[...] = split3(w_ref[...], 0)
-
-    pl.semaphore_wait(barrier, chips)
 
     def spread(source, slot, sems):
         return [remote(source, slot(1), sems.at[0, 1], sems.at[1, 1], sister)] + [
@@ -215,8 +238,6 @@
         ]
 
     about_slot = lambda b: about.at[b]
-    quarters = people // quarter
-
     def other_slot(q):
         return lambda b: others.at[b - 1, q]
 
@@ -226,17 +247,11 @@
     ]
     about_relay = relay(about_slot, about_sems)
     other_relay = [relay(other_slot(q), other_sems.at[q]) for q in range(quarters)]
-    for copy in about_copies[1:] + about_copies[:1]:
-        copy.start()
-
     def start_over_y(first, last):
         for q in range(first, last):
             for copy in other_copies[q][1:]:
                 copy.start()
 
-    start_over_y(0, quarters // 2)
-    for q in range(quarters):
-        other_copies[q][0].start()
 
     cut = offsets[1, 2] // lanes
     chunks = [(0, cut), (cut, tiles)]
@@ -304,32 +319,34 @@
 
         each_other(chips, start)
 
-    def smooth_part(b, first, last):
+    def smooth_part(b):
         if b > 0:
-            value = about[b].astype(f32)
-            located[b, :, : people // 2] = value[: value.shape[0] // 2]
-            located[b, :, people // 2 :] = value[value.shape[0] // 2 :]
-
-        def body(i, carry):
-            start = pl.multiple_of(i * smooth_block, smooth_block)
-            cols = pl.ds(start, smooth_block)
-            there = pl.ds(pl.multiple_of(b * people + start, smooth_block), smooth_block)
-            income = located[b, variables + 1 : variables + 2, cols] * half_scale
-            centers = jnp.concatenate([cen[...]] * (smooth_block // lanes), axis=1)
-            smooth[:, there] = (0.5 + 0.5 * jnp.tanh(centers - income)).astype(bf16)
+            for q in range(quarters // 2):
+                value = about[b, :, q * quarter : (q + 1) * quarter].astype(f32)
+                located[b * quarters + q] = value[:8]
+                located[b * quarters + quarters // 2 + q] = value[8:]
+
+        def body(q, carry):
+            c = b * quarters + q
+            income = located[c, variables + 1 : variables + 2, :] * half_scale
+            for i in range(quarter // lanes):
+                at = slice(i * lanes, (i + 1) * lanes)
+                smooth[c, :, at] = (0.5 + 0.5 * jnp.tanh(cen[...] - income[:, at])).astype(bf16)
             for v in range(variables):
-                code = located[b, v : v + 1, cols].astype(jnp.int32)
-                design[v * base_levels : (v + 1) * base_levels, there] = one_hot(code, base_levels)
+                code = located[c, v : v + 1, :].astype(jnp.int32)
+                design[c, v * base_levels : (v + 1) * base_levels, :] = one_hot(code, base_levels)
             return carry
 
-        lax.fori_loop(first, last, body, 0)
-
-    steps = people // smooth_block
+        lax.fori_loop(0, quarters, body, 0)
 
     gram_chunk(*chunks[0])
+    gram_chunk(*chunks[1])
+    pl.semaphore_wait(barrier, chips)
     to_sister(0).start()
-    gram_chunk(*chunks[1])
     to_sister(1).start()
+    for copy in about_copies[1:] + about_copies[:1]:
+        copy.start()
+    start_over_y(0, quarters // 2)
     to_chips(0)
 
     corner[...] = jnp.zeros_like(corner)
@@ -338,13 +355,18 @@
         (grid_ref[pl.ds(rec * count, count), :].astype(f32) - grid_middle)
         * (grid_step * half_scale)
     )
+    corner[count : count + 1, : controls_ref.shape[1]] = controls_ref[...]
     turned = corner[...].T
     for i in range(count):
         cen[i * lanes : (i + 1) * lanes, :] = jnp.broadcast_to(turned[:, i : i + 1], (lanes, lanes))
 
+    size = mat.shape[0]
+    aims = jnp.broadcast_to(turned[:size, count : count + 1], (size, reps))
     to_chips(1)
     start_over_y(quarters // 2, quarters - 1)
-    smooth_part(0, 0, steps)
+    for q in range(quarters):
+        other_copies[q][0].start()
+    smooth_part(0)
     for e in range(1, ny):
         about_copies[e].wait_recv()
         about_relay[e - 1].start()
@@ -376,7 +398,7 @@
         )
 
     about_copies[0].wait_recv()
-    smooth_part(1, 0, steps)
+    smooth_part(1)
 
     def hand_over(t):
         return remote(
@@ -402,105 +424,145 @@
         hand_over(t).start()
     start_over_y(quarters - 1, quarters)
     for e in range(1, ny):
-        smooth_part(2 * e, 0, steps)
+        smooth_part(2 * e)
         about_relay[e - 1].wait_recv()
-        smooth_part(2 * e + 1, 0, steps)
+        smooth_part(2 * e + 1)
     for t in range(tiles):
         taken(t).wait_recv()
         whole = jnp.concatenate([final[0, t], final[1, t]], axis=0)
         sums[t * lanes : (t + 1) * lanes, :] = whole.T
 
-    x3[...] = split3(solve(variables, sums, controls_ref, mat, rhs, coef, sol), 0)
-
-    for q in range(quarters):
-        for e in range(1, ny):
-            other_copies[q][e].wait_recv()
-            other_relay[q][e - 1].start()
-
-    def table_pass(part):
-        table[part] = jnp.zeros(table.shape[1:], f32)
-        for b in range(blocks):
-            if part == 0 and b > 0:
-                if b % 2 == 1:
-                    for q in range(quarters):
-                        (other_copies[q][0] if b == 1 else other_relay[q][b // 2 - 1]).wait_recv()
-
-            def body(i, carry, b=b):
-                start = pl.multiple_of(i * table_block, table_block)
-                cols = pl.ds(start, table_block)
-                there = pl.ds(pl.multiple_of(b * people + start, table_block), table_block)
-                if part == 0:
-                    adjustment = lax.dot_general(
-                        x3[...],
-                        jnp.concatenate([design[:, there]] * 3, axis=0),
-                        (((0,), (0,)), ((), ())),
-                        preferred_element_type=f32,
-                    )
-                    if b == 0:
-                        weights = w_ref[:, cols]
-                    else:
-                        code = others[b - 1, i].astype(jnp.int32).astype(f32)
-                        weights = (code + 32768.0) * code_step + low_weight
-                    calibrated = weights * (1.0 + adjustment)
-                    if b == 0:
-                        cal_ref[:, cols] = calibrated
-                    sent[:, there] = calibrated.astype(bf16)
-                own = located[b, variables : variables + 1, cols]
-                value = sent[:, there]
-                for k in range(tracts):
-                    at = (k % nx * nz + k // nx) * reps
-                    inside = jnp.where(own == float(k), 1.0, 0.0).astype(bf16)
-                    masked[at : at + reps, :] = value * inside
-                table[part] += lax.dot_general(
-                    masked[...],
-                    smooth[part * width : (part + 1) * width, there],
-                    (((1,), (1,)), ((), ())),
-                    preferred_element_type=f32,
-                )
-                return carry
-
-            lax.fori_loop(0, people // table_block, body, 0)
-
-    deep = nz * reps
-
-    def across_x(part, e):
-        to = lax.rem(x + e, nx)
+    def relay_over_y(first, last):
+        for q in range(first, last):
+            for e in range(1, ny):
+                other_copies[q][e].wait_recv()
+                other_relay[q][e - 1].start()
+
+    relay_over_y(0, quarters // 2)
+    x3[...] = split3(solve(variables, sums, aims, mat, rhs, coef, sol), 0)
+    relay_over_y(quarters // 2, quarters)
+
+    def factors(c):
+        return 1.0 + lax.dot_general(
+            x3[...],
+            jnp.concatenate([design[c]] * 3, axis=0),
+            (((0,), (0,)), ((), ())),
+            preferred_element_type=f32,
+        )
+
+    def own_weights(q, carry):
+        cols = pl.ds(pl.multiple_of(q * quarter, quarter), quarter)
+        factor = factors(q)
+        cal_ref[:, cols] = factor
+        sent[q] = (w_ref[:, cols] * factor).astype(bf16)
+        return carry
+
+    lax.fori_loop(0, quarters, own_weights, 0)
+
+    def other_weights(b, q):
+        code = others[b - 1, q].astype(jnp.int32).astype(f32)
+        weights = (code + 32768.0) * code_step + low_weight
+        sent[b * quarters + q] = (weights * factors(b * quarters + q)).astype(bf16)
+
+    halves = pieces_j // 2
+
+    def mask(c, e, target):
+        own = located[c, variables : variables + 1, :]
+        value = sent[c]
+        for k in range(nz):
+            place = (k * nx + lax.rem(x + e, nx)).astype(f32)
+            inside = jnp.where(own == place, 1.0, 0.0).astype(bf16)
+            target[k * reps : (k + 1) * reps, :] = value * inside
+
+    def add_product(c, source, e, first, count):
+        product = lax.dot_general(
+            source[...],
+            smooth[c, first * lanes : (first + count) * lanes, :],
+            (((1,), (1,)), ((), ())),
+            preferred_element_type=f32,
+        )
+        for j in range(count):
+            table[e, first + j] += product[:, j * lanes : (j + 1) * lanes]
+
+    last = blocks * quarters - 1
+
+    def table_loop(e, first, count, low, high, b=None):
+        def body(i, carry):
+            c = 2 * i
+            add_product(c, masked, e, first, count)
+            mask(c + 1, e, masked_too)
+            if b is not None:
+                other_weights(b, c - (b - 1) * quarters)
+            add_product(c + 1, masked_too, e, first, count)
+            if b is not None:
+                other_weights(b, c + 1 - (b - 1) * quarters)
+            mask(jnp.minimum(c + 2, last), e, masked)
+            return carry
+
+        lax.fori_loop(low // 2, high // 2, body, 0)
+
+    def across_x(e, j):
         return remote(
-            table.at[part, pl.ds(pl.multiple_of(to * deep, 8), deep)],
-            from_x.at[part, e - 1],
-            x_sems.at[0, part, e],
-            x_sems.at[1, part, e],
-            {"tract": z * nx + to},
-        )
-
-    def along_z(part, e):
-        to = lax.rem(z + e, nz)
+            to_x.at[e - 1, j],
+            from_x.at[e - 1, j],
+            x_sems.at[0, e - 1, j],
+            x_sems.at[1, e - 1, j],
+            {"tract": z * nx + lax.rem(x + e, nx)},
+        )
+
+    def along_z(e, j):
         return remote(
-            over_x.at[part, pl.ds(pl.multiple_of(to * reps, 8), reps)],
-            from_z.at[part, e - 1],
-            z_sems.at[0, part, e],
-            z_sems.at[1, part, e],
-            {"tract": to * nx + x},
-        )
-
+            to_z.at[e - 1, j],
+            from_z.at[e - 1, j],
+            z_sems.at[0, e - 1, j],
+            z_sems.at[1, e - 1, j],
+            {"tract": lax.rem(z + e, nz) * nx + x},
+        )
+
+    def send_over_x(e, part):
+        for j in range(part * halves, (part + 1) * halves):
+            for k in range(nz):
+                to_x[e - 1, j, k] = encode(table[e, j, k * reps : (k + 1) * reps, :])
+            across_x(e, j).start()
+
+    def send_along_z(part):
+        for j in range(part * halves, (part + 1) * halves):
+            for e in range(1, nx):
+                across_x(e, j).wait_recv()
+            for k in range(nz):
+                value = table[0, j, k * reps : (k + 1) * reps, :]
+                for e in range(1, nx):
+                    value = value + decode(from_x[e - 1, j, k])
+                over_x[j, k] = value
+            for e in range(1, nz):
+                to_z[e - 1, j] = encode(over_x[j, lax.rem(z + e, nz)])
+                along_z(e, j).start()
+
+    table[...] = jnp.zeros_like(table)
+    for e in range(1, nx):
+        for part in range(2):
+            mask(0, e, masked)
+            if e > 1 or part > 0:
+                table_loop(e, part * halves, halves, 0, blocks * quarters)
+            else:
+                for b in range(blocks):
+                    if b + 1 < blocks and (b + 1) % 2 == 1:
+                        for q in range(quarters):
+                            arrived = other_copies[q][0] if b == 0 else other_relay[q][b // 2 - 1]
+                            arrived.wait_recv()
+                    following = b + 1 if b + 1 < blocks else None
+                    table_loop(e, 0, halves, b * quarters, (b + 1) * quarters, following)
+            send_over_x(e, part)
     for part in range(2):
-        table_pass(part)
-        for e in range(1, nx):
-            across_x(part, e).start()
-    for part in range(2):
-        value = table[part, pl.ds(pl.multiple_of(x * deep, 8), deep), :]
-        for e in range(1, nx):
-            across_x(part, e).wait_recv()
-            value = value + from_x[part, e - 1]
-        over_x[part] = value
+        mask(0, 0, masked)
+        table_loop(0, part * halves, halves, 0, blocks * quarters)
+        send_along_z(part)
+    for j in range(pieces_j):
+        value = over_x[j, z]
         for e in range(1, nz):
-            along_z(part, e).start()
-    for part in range(2):
-        value = over_x[part, pl.ds(pl.multiple_of(z * reps, 8), reps), :]
-        for e in range(1, nz):
-            along_z(part, e).wait_recv()
-            value = value + from_z[part, e - 1]
-        tab_ref[0, :, part * width : (part + 1) * width] = value / scale
+            along_z(e, j).wait_recv()
+            value = value + decode(from_z[e - 1, j])
+        tab_ref[0, :, j * lanes : (j + 1) * lanes] = value
 
     for copy in about_copies + about_relay + sum(other_copies + other_relay, []):
         copy.wait_send()
@@ -525,11 +587,11 @@
     each_other(chips, left)
     for t in range(tiles):
         hand_over(t).wait_send()
-    for part in range(2):
+    for j in range(pieces_j):
         for e in range(1, nx):
-            across_x(part, e).wait_send()
+            across_x(e, j).wait_send()
         for e in range(1, nz):
-            along_z(part, e).wait_send()
+            along_z(e, j).wait_send()
 
 
 def shards(rep_weights, covariate_codes, tract_of, log_income, controls, threshold_grid):
@@ -542,7 +604,8 @@
     nx = tracts // nz
     chips = ny * tracts
     share = threshold_grid.shape[0] // recs
-    width = share // 2
+    pieces_j = share // lanes
+    quarters = people // quarter
     size = controls.shape[0]
     rows = pair_layout(variables)[2]
     tiles = -(-rows // lanes)
@@ -551,8 +614,8 @@
     designs = variables * base_levels
     vmem = pltpu.VMEM
     dma = pltpu.SemaphoreType.DMA
-    return pl.pallas_call(
-        functools.partial(kernel, ny, tracts, nx, float(people * recs)),
+    factor, tables = pl.pallas_call(
+        functools.partial(kernel, ny, tracts, nx),
         in_specs=[pl.BlockSpec(memory_space=vmem)] * 6,
         out_specs=[pl.BlockSpec(memory_space=vmem)] * 2,
         out_shape=[
@@ -576,17 +639,20 @@
             vmem((recs, 16, people // 2), bf16),
             vmem((people // quarter, reps, quarter), jnp.int16),
             vmem((recs - 1, people // quarter, reps, quarter), jnp.int16),
-            vmem((recs, 8, people), f32),
+            vmem((recs * quarters, 8, quarter), f32),
             vmem((8, lanes), f32),
             vmem((share, lanes), f32),
-            vmem((share, recs * people), bf16),
-            vmem((designs, recs * people), bf16),
-            vmem((reps, recs * people), bf16),
-            vmem((tracts * reps, table_block), bf16),
-            vmem((2, tracts * reps, width), f32),
-            vmem((2, nx - 1, nz * reps, width), f32),
-            vmem((2, nz * reps, width), f32),
-            vmem((2, nz - 1, reps, width), f32),
+            vmem((recs * quarters, share, quarter), bf16),
+            vmem((recs * quarters, designs, quarter), bf16),
+            vmem((recs * quarters, reps, quarter), bf16),
+            vmem((nz * reps, quarter), bf16),
+            vmem((nz * reps, quarter), bf16),
+            vmem((nx, pieces_j, nz * reps, lanes), f32),
+            vmem((nx - 1, pieces_j, nz, reps + 16, lanes), jnp.int16),
+            vmem((nx - 1, pieces_j, nz, reps + 16, lanes), jnp.int16),
+            vmem((pieces_j, nz, reps, lanes), f32),
+            vmem((nz - 1, pieces_j, reps + 16, lanes), jnp.int16),
+            vmem((nz - 1, pieces_j, reps + 16, lanes), jnp.int16),
             dma((2, recs)),
             dma((people // quarter, 2, recs)),
             dma((2, 2)),
@@ -595,8 +661,8 @@
             dma((chips,)),
             dma((tiles,)),
             dma((2, tiles)),
-            dma((2, 2, nx)),
-            dma((2, 2, nz)),
+            dma((2, nx - 1, pieces_j)),
+            dma((2, nz - 1, pieces_j)),
         ],
         compiler_params=pltpu.CompilerParams(
             vmem_limit_bytes=vmem_bytes, collective_id=0, has_side_effects=True
@@ -605,10 +671,11 @@
         rep_weights,
         covariate_codes,
         tract_of.reshape(1, people),
-        log_income.astype(f32).reshape(1, people),
-        jnp.broadcast_to(controls[:, None], (size, reps)),
+        log_income.reshape(-1, lanes),
+        controls.reshape(1, size),
         threshold_grid.reshape(-1, lanes),
     )
+    return rep_weights * factor, tables / float(people * recs)
 
 
 def solution(mesh):

time: 82.7 us -> 78.2 us (0.946)
  local copies, waits for them, and re-layouts: 4.52 us -> 0.01 us
  other arithmetic: 1.3 us -> 3.22 us
  Pallas kernels: 76 us -> 74.1 us
    unnamed x4, local copies, waits for them, and re-layouts: 3.18 us -> 0.01 us
    mul x0 -> x1, other arithmetic: none -> 2.54 us  [shards(): return (rep_weights * factor, tables / float(people * recs))]
    pallas_call x1, Pallas kernels: 76 us -> 74.1 us  [shards(): pl.pallas_call(functools.partial(kernel, ny, tracts, nx), in_specs=[pl.Bl...]
    broadcast_in_dim x1 -> x0, local copies, waits for them, and re-layouts: 1.34 us -> none  [shards(): jnp.broadcast_to(controls[:, None], (size, reps))]
    reshape x1 -> x0, other arithmetic: 1.3 us -> none  [shards(): log_income.astype(f32).reshape(1, people)]
where the time goes in v3:
time: 78.2 us; the launch traced here: 78 us
  Pallas kernels  74.1 us (95%)
  other arithmetic  3.22 us (4%)
    pallas_call x1, Pallas kernels, shards(): pl.pallas_call(functools.partial(kernel, ny, tracts, nx), in_specs=[pl.Bl...  74.1 us
    mul x1, other arithmetic, shards(): return (rep_weights * factor, tables / float(people * recs))  2.54 us

profile of v3, /device:TPU:0, one launch (start us, length us, event | category | flops | bytes accessed | tf_op | source)
XLA Modules:
  0.0 78.0 jit_solution(9357490615579706221)
XLA Ops:
  0.6 0.0 copy-start
  0.6 74.1 %shard_map.77 = (f32[80,4096]{1,0:T(8,128)}, f32[1,80,512]{2,1,0:T(8,128)}) custom-call(f32[80,4096]{1,0:T(8,128)} %w_ref.1, s32[5,4096]{1,0:T(8,128)} %codes_ref.1, s32[1,4096]{1,0:T(1,128)} %bitcast.4, bf16[32,128]{1,0:T(8,128)(2,1)} %bitcast.5, f32[1,64]{1,0:T(1,128)} %bitcast.7, s32[16,128]{1,0:T(8,128)} %bitcast.6), custom_call_target="tpu_custom_call" | custom-call | tf_op jit(solution)/shard_map/pallas_call | solution.py:617
  74.8 0.0 copy-done
  74.8 0.0 copy-start.1
  74.8 2.5 %mul.3 = f32[80,4096]{1,0:T(8,128)} multiply(f32[80,4096]{1,0:T(8,128)S(1)} %copy-done, f32[80,4096]{1,0:T(8,128)} %get-tuple-element.4) | non-fusion elementwise | flops 327680 | bytes 3932160 | tf_op jit(solution)/shard_map/mul | solution.py:678
  77.3 0.0 copy-done.1
  77.4 0.7 broadcast_multiply_fusion
Async XLA Ops:
  0.6 74.2 %copy-start = (f32[80,4096]{1,0:T(8,128)S(1)}, f32[80,4096]{1,0:T(8,128)}, u32[]{:S(2)}) copy-start(f32[80,4096]{1,0:T(8,128)} %w_ref.1) | copy-start | bytes 3932164
  74.8 2.6 %copy-start.1 = (f32[1,80,512]{2,1,0:T(8,128)S(1)}, f32[1,80,512]{2,1,0:T(8,128)}, u32[]{:S(2)}) copy-start(f32[1,80,512]{2,1,0:T(8,128)} %get-tuple-element.5) | copy-start | bytes 491524

commit v4 on v3

--- a/solution.py
+++ b/solution.py
@@ -96,36 +96,47 @@
             at = row + c * kept
             mat[starts[u] + c, starts[v] : starts[v] + kept, :] = sums[at : at + kept, :]
 
-    for block in range(size // 8):
-        low = block * 8
-
-        def eliminate(inner, carry, low=low, block=block):
-            k = low + inner
-            row = mat[k, low:, :]
-            pivot = mat[k, pl.ds(k, 1), :]
-            place = lax.broadcasted_iota(jnp.int32, row.shape, 0) + low
-            factor = jnp.where(place > k, row * (1.0 / pivot), 0.0)
-            coef[low:, :] = factor
-            rhs[low:, :] = rhs[low:, :] - factor * rhs[pl.ds(k, 1), :]
-            for other in range(block, size // 8):
-                part = row[other * 8 - low :, :]
-                for i in range(other * 8, other * 8 + 8):
-                    mat[i, other * 8 :, :] = mat[i, other * 8 :, :] - coef[i : i + 1, :] * part
-            return carry
-
-        lax.fori_loop(0, 8, eliminate, 0)
-
-    sol[...] = jnp.zeros_like(sol)
-    for block in reversed(range(size // 8)):
-        low = block * 8
-
-        def substitute(inner, carry, low=low):
-            k = low + 7 - inner
-            known = jnp.sum(mat[k, low:, :] * sol[low:, :], axis=0, keepdims=True)
-            sol[pl.ds(k, 1), :] = (rhs[pl.ds(k, 1), :] - known) / mat[k, pl.ds(k, 1), :]
-            return carry
-
-        lax.fori_loop(0, 8, substitute, 0)
+    inverses = []
+    for low in range(0, size, 8):
+        rows = [mat[low + p, low:, :] for p in range(8)]
+        right = rhs[low:, :]
+        place = lax.broadcasted_iota(jnp.int32, rows[0].shape, 0)
+        for p in range(8):
+            inverse = 1.0 / rows[p][p : p + 1, :]
+            factor = jnp.where(place > p, rows[p] * inverse, 0.0)
+            coef[p, low:, :] = factor
+            for q in range(p + 1, 8):
+                rows[q] = rows[q] - factor[q : q + 1, :] * rows[p]
+            right = right - factor * right[p : p + 1, :]
+            inverses.append(inverse)
+        rhs[low:, :] = right
+        for p in range(8):
+            mat[low + p, low:, :] = rows[p]
+        for other in range(low + 8, size, 8):
+
+            def update(pair, carry, low=low, other=other):
+                for i in (other + 2 * pair, other + 2 * pair + 1):
+                    value = mat[i, other:, :]
+                    for p in range(8):
+                        value = value - coef[p, pl.ds(i, 1), :] * mat[low + p, other:, :]
+                    mat[i, other:, :] = value
+                return carry
+
+            lax.fori_loop(0, 4, update, 0)
+
+    for low in reversed(range(0, size, 8)):
+        known = []
+        for p in range(8):
+            value = rhs[low + p : low + p + 1, :]
+            if low + 8 < size:
+                later = mat[low + p, low + 8 :, :] * sol[low + 8 :, :]
+                value = value - jnp.sum(later, axis=0, keepdims=True)
+            known.append(value)
+        for p in reversed(range(8)):
+            found = known[p] * inverses[low + p]
+            sol[low + p : low + p + 1, :] = found
+            for q in range(p):
+                known[q] = known[q] - mat[low + q, low + p : low + p + 1, :] * found
 
     parts = []
     for v in range(variables):
@@ -144,9 +155,10 @@
 
 
 def kernel(
-    ny, tracts, nx,
-    w_ref, codes_ref, tract_ref, income_ref, controls_ref, grid_ref,
-    cal_ref, tab_ref,
+    ny, tracts, nx, scale,
+    w_hbm, codes_ref, tract_ref, income_ref, controls_ref, grid_ref,
+    cal_hbm, tab_hbm,
+    w_ref, tab_ref, w_sems, cal_sem, tab_sem,
     pieces, pairs, acc, gram, from_sister, from_chip, final, sums, mat, rhs, coef, sol, x3,
     about, coded, others, located, corner, cen, smooth, design, sent, masked, masked_too, table,
     to_x, from_x, over_x, to_z, from_z,
@@ -155,6 +167,7 @@
 ):
     reps, people = w_ref.shape
     variables = codes_ref.shape[0]
+    quarters = people // quarter
     nz = tracts // nx
     blocks = 2 * ny
     chips = ny * tracts
@@ -164,7 +177,17 @@
     firsts = firsts_of(variables)
     share = smooth.shape[1]
     pieces_j = share // lanes
-    quarters = people // quarter
+
+    loads = [
+        pltpu.make_async_copy(
+            w_hbm.at[:, q * quarter : (q + 1) * quarter],
+            w_ref.at[:, q * quarter : (q + 1) * quarter],
+            w_sems.at[q],
+        )
+        for q in range(quarters)
+    ]
+    for load in loads:
+        load.start()
 
     rec, tract = lax.axis_index("rec"), lax.axis_index("tract")
     y, core = lax.div(rec, 2), lax.rem(rec, 2)
@@ -213,6 +236,7 @@
             [located[q], located[quarters // 2 + q]], axis=0
         ).astype(bf16)
     for q in range(quarters):
+        loads[q].wait()
         part = w_ref[:, q * quarter : (q + 1) * quarter]
         coded[q] = jnp.round((part - low_weight) / code_step - 32768.0).astype(jnp.int32).astype(jnp.int16)
     pieces[...] = split3(w_ref[...], 0)
@@ -346,7 +370,7 @@
     to_sister(1).start()
     for copy in about_copies[1:] + about_copies[:1]:
         copy.start()
-    start_over_y(0, quarters // 2)
+    start_over_y(0, 1)
     to_chips(0)
 
     corner[...] = jnp.zeros_like(corner)
@@ -363,9 +387,7 @@
     size = mat.shape[0]
     aims = jnp.broadcast_to(turned[:size, count : count + 1], (size, reps))
     to_chips(1)
-    start_over_y(quarters // 2, quarters - 1)
-    for q in range(quarters):
-        other_copies[q][0].start()
+    start_over_y(1, quarters // 2)
     smooth_part(0)
     for e in range(1, ny):
         about_copies[e].wait_recv()
@@ -422,7 +444,9 @@
             ).wait_recv()
 
         hand_over(t).start()
-    start_over_y(quarters - 1, quarters)
+    start_over_y(quarters // 2, quarters)
+    for q in range(quarters):
+        other_copies[q][0].start()
     for e in range(1, ny):
         smooth_part(2 * e)
         about_relay[e - 1].wait_recv()
@@ -452,12 +476,14 @@
 
     def own_weights(q, carry):
         cols = pl.ds(pl.multiple_of(q * quarter, quarter), quarter)
-        factor = factors(q)
-        cal_ref[:, cols] = factor
-        sent[q] = (w_ref[:, cols] * factor).astype(bf16)
+        calibrated = w_ref[:, cols] * factors(q)
+        w_ref[:, cols] = calibrated
+        sent[q] = calibrated.astype(bf16)
         return carry
 
     lax.fori_loop(0, quarters, own_weights, 0)
+    cal_copy = pltpu.make_async_copy(w_ref, cal_hbm, cal_sem)
+    cal_copy.start()
 
     def other_weights(b, q):
         code = others[b - 1, q].astype(jnp.int32).astype(f32)
@@ -562,8 +588,12 @@
         for e in range(1, nz):
             along_z(e, j).wait_recv()
             value = value + decode(from_z[e - 1, j])
-        tab_ref[0, :, j * lanes : (j + 1) * lanes] = value
-
+        tab_ref[0, :, j * lanes : (j + 1) * lanes] = value / scale
+    tab_copy = pltpu.make_async_copy(tab_ref, tab_hbm, tab_sem)
+    tab_copy.start()
+
+    cal_copy.wait()
+    tab_copy.wait()
     for copy in about_copies + about_relay + sum(other_copies + other_relay, []):
         copy.wait_send()
     for c in range(2):
@@ -592,6 +622,43 @@
             across_x(e, j).wait_send()
         for e in range(1, nz):
             along_z(e, j).wait_send()
+
+
+def finish_kernel(cal_ref, tab_ref, cal_out, tab_out, cal, tab, sems):
+    reps = cal_ref.shape[0]
+    copy = pltpu.make_async_copy
+    arriving, leaving = [], []
+    for first in range(0, reps, 8):
+        rows, at = slice(first, first + 8), first // 8
+        arriving.append(copy(cal_ref.at[rows], cal.at[rows], sems.at[0, at]))
+        leaving.append(copy(cal.at[rows], cal_out.at[rows], sems.at[1, at]))
+    arriving.append(copy(tab_ref, tab, sems.at[0, reps // 8]))
+    leaving.append(copy(tab, tab_out, sems.at[1, reps // 8]))
+    for come in arriving:
+        come.start()
+    for come, go in zip(arriving, leaving):
+        come.wait()
+        go.start()
+    for go in leaving:
+        go.wait()
+
+
+def finish(calibrated, tables):
+    return pl.pallas_call(
+        finish_kernel,
+        in_specs=[pl.BlockSpec(memory_space=pltpu.HBM)] * 2,
+        out_specs=[pl.BlockSpec(memory_space=pltpu.HBM)] * 2,
+        out_shape=[
+            jax.ShapeDtypeStruct(calibrated.shape, f32),
+            jax.ShapeDtypeStruct(tables.shape, f32),
+        ],
+        scratch_shapes=[
+            pltpu.VMEM(calibrated.shape, f32),
+            pltpu.VMEM(tables.shape, f32),
+            pltpu.SemaphoreType.DMA((2, calibrated.shape[0] // 8 + 1)),
+        ],
+        compiler_params=pltpu.CompilerParams(vmem_limit_bytes=vmem_bytes),
+    )(calibrated, tables)
 
 
 def shards(rep_weights, covariate_codes, tract_of, log_income, controls, threshold_grid):
@@ -614,15 +681,20 @@
     designs = variables * base_levels
     vmem = pltpu.VMEM
     dma = pltpu.SemaphoreType.DMA
-    factor, tables = pl.pallas_call(
-        functools.partial(kernel, ny, tracts, nx),
-        in_specs=[pl.BlockSpec(memory_space=vmem)] * 6,
-        out_specs=[pl.BlockSpec(memory_space=vmem)] * 2,
+    calibrated, tables = pl.pallas_call(
+        functools.partial(kernel, ny, tracts, nx, float(people * recs)),
+        in_specs=[pl.BlockSpec(memory_space=pltpu.HBM)] + [pl.BlockSpec(memory_space=vmem)] * 5,
+        out_specs=[pl.BlockSpec(memory_space=pltpu.HBM)] * 2,
         out_shape=[
             jax.ShapeDtypeStruct((reps, people), f32),
             jax.ShapeDtypeStruct((1, reps, share), f32),
         ],
         scratch_shapes=[
+            vmem((reps, people), f32),
+            vmem((1, reps, share), f32),
+            dma((quarters,)),
+            dma,
+            dma,
             vmem((3 * reps, people), bf16),
             vmem((most, gram_block), bf16),
             vmem((3 * reps, most), f32),
@@ -633,7 +705,7 @@
             vmem((tiles * lanes, reps), f32),
             vmem((size, size, reps), f32),
             vmem((size, reps), f32),
-            vmem((size, reps), f32),
+            vmem((8, size, reps), f32),
             vmem((size, reps), f32),
             vmem((3 * designs, reps), bf16),
             vmem((recs, 16, people // 2), bf16),
@@ -675,7 +747,7 @@
         controls.reshape(1, size),
         threshold_grid.reshape(-1, lanes),
     )
-    return rep_weights * factor, tables / float(people * recs)
+    return finish(calibrated, tables)
 
 
 def solution(mesh):

time: 78.2 us -> 72.8 us (0.931)
  other arithmetic: 3.22 us -> 0 us
  Pallas kernels: 74.1 us -> 71.8 us
    mul x1 -> x0, other arithmetic: 2.54 us -> none  [shards(): return (rep_weights * factor, tables / float(people * recs))]
    pallas_call x1 -> x2, Pallas kernels: 74.1 us -> 71.8 us  [the longest x1 69.5 us: shards(): pl.pallas_call(functools.partial(kernel, ny, tracts, nx, float(people * r...]
where the time goes in v4:
time: 72.8 us; the launch traced here: 72.6 us
  Pallas kernels  71.8 us (99%)
  between operations  0.8 us (1%)
    pallas_call x1, Pallas kernels, shards(): pl.pallas_call(functools.partial(kernel, ny, tracts, nx, float(people * r...  69.5 us
    pallas_call x1, Pallas kernels, finish(): pl.pallas_call(finish_kernel, in_specs=[pl.BlockSpec(memory_space=pltpu.H...  2.28 us

profile of v4, /device:TPU:0, one launch (start us, length us, event | category | flops | bytes accessed | tf_op | source)
XLA Modules:
  0.0 72.6 jit_solution(16473764182133765522)
XLA Ops:
  0.6 69.5 %shard_map.77 = (f32[80,4096]{1,0:T(8,128)}, f32[1,80,512]{2,1,0:T(8,128)}) custom-call(f32[80,4096]{1,0:T(8,128)} %w_hbm.1, s32[5,4096]{1,0:T(8,128)} %codes_ref.1, s32[1,4096]{1,0:T(1,128)} %bitcast.4, bf16[32,128]{1,0:T(8,128)(2,1)} %bitcast.5, f32[1,64]{1,0:T(1,128)} %bitcast.7, s32[16,128]{1,0:T(8,128)} %bitcast.6), custom_call_target="tpu_custom_call" | custom-call | tf_op jit(solution)/shard_map/pallas_call | solution.py:684
  70.1 2.3 %shard_map.78 = (f32[80,4096]{1,0:T(8,128)}, f32[1,80,512]{2,1,0:T(8,128)}) custom-call(f32[80,4096]{1,0:T(8,128)} %get-tuple-element.4.cal_ref, f32[1,80,512]{2,1,0:T(8,128)} %get-tuple-element.5.tab_ref), custom_call_target="tpu_custom_call" | custom-call | tf_op jit(solution)/shard_map/pallas_call | solution.py:647

commit v5 on v4

--- a/solution.py
+++ b/solution.py
@@ -481,7 +481,7 @@
         sent[q] = calibrated.astype(bf16)
         return carry
 
-    lax.fori_loop(0, quarters, own_weights, 0)
+    lax.fori_loop(0, quarters, own_weights, 0, unroll=True)
     cal_copy = pltpu.make_async_copy(w_ref, cal_hbm, cal_sem)
     cal_copy.start()
 

time: 72.8 us -> 72.2 us (level)
  no operation moved by 1% of the time
where the time goes in v5:
time: 72.2 us; the launch traced here: 72 us
  Pallas kernels  71.2 us (99%)
  between operations  0.8 us (1%)
    pallas_call x1, Pallas kernels, shards(): pl.pallas_call(functools.partial(kernel, ny, tracts, nx, float(people * r...  68.9 us
    pallas_call x1, Pallas kernels, finish(): pl.pallas_call(finish_kernel, in_specs=[pl.BlockSpec(memory_space=pltpu.H...  2.28 us

profile of v5, /device:TPU:0, one launch (start us, length us, event | category | flops | bytes accessed | tf_op | source)
XLA Modules:
  0.0 72.0 jit_solution(8529027778204768413)
XLA Ops:
  0.6 68.9 %shard_map.77 = (f32[80,4096]{1,0:T(8,128)}, f32[1,80,512]{2,1,0:T(8,128)}) custom-call(f32[80,4096]{1,0:T(8,128)} %w_hbm.1, s32[5,4096]{1,0:T(8,128)} %codes_ref.1, s32[1,4096]{1,0:T(1,128)} %bitcast.4, bf16[32,128]{1,0:T(8,128)(2,1)} %bitcast.5, f32[1,64]{1,0:T(1,128)} %bitcast.7, s32[16,128]{1,0:T(8,128)} %bitcast.6), custom_call_target="tpu_custom_call" | custom-call | tf_op jit(solution)/shard_map/pallas_call | solution.py:684
  69.6 2.3 %shard_map.78 = (f32[80,4096]{1,0:T(8,128)}, f32[1,80,512]{2,1,0:T(8,128)}) custom-call(f32[80,4096]{1,0:T(8,128)} %get-tuple-element.4.cal_ref, f32[1,80,512]{2,1,0:T(8,128)} %get-tuple-element.5.tab_ref), custom_call_target="tpu_custom_call" | custom-call | tf_op jit(solution)/shard_map/pallas_call | solution.py:647
